TPU v7x, 32 devices: a whole 2x2x4 slice. The times are simulated.
32 devices in a mesh: frame: 4 (over y, core), tile: 8 (over z, x).
Axes of the slice: x: 2, y: 2, z: 4, core: 2. Of those that a mesh axis runs over, the one named last changes fastest.
Arguments:
- movie: bfloat16 [32, 2, 512, 512], P('frame', None, 'tile'), may hold values from -6 to 6
- shifts: int32 [32, 2], P('frame'), may hold values from -8 to 8, as said below
- filters: float32 [2, 64], replicated, may hold values from -0.5 to 0.5
- weights: bfloat16 [1024, 16384], P(('frame', 'tile')), may hold values from -0.046875 to 0.046875
- slot_owner: int32 [1024, 1], P(('frame', 'tile')), may hold values from 0 to 31; in each aligned block of 32 rows (0 to 31, 32 to 63, ...) at most 2 rows name the same one
- slot_local: int32 [1024, 1], P(('frame', 'tile')), may hold values from 0 to 31
Outputs:
- traces: float32 [1024, 32], P(('frame', 'tile'))
Inputs may be any that keep to these rules, and one draw needn't show every extreme that they name: `shifts`: each offset has magnitude at most 8; a row offset of 8 and one of -8 occur in every draw. `slot_owner`: among the 32 entries of one pixel tile no owner is named more than 2 times.
All inputs are finite; a program needn't handle non-finite values.
Results may differ from a plain program's by a relative error of at most 0.0047.
Values may be sent and summed in bfloat16 or wider, within the bound.
No kernel may reach another device: no remote copies, remote signals or barrier semaphores. Data moves between devices by JAX's collectives and lax.ppermute only.
A program may use at most 128 MiB of HBM per device.

v0:
```python
import functools

import jax
import jax.numpy as jnp
import numpy as np
from jax import lax
from jax.experimental import pallas as pl
from jax.experimental.pallas import tpu as pltpu
from jax.sharding import PartitionSpec as P

COMP_DEV = 32
TAPS = 64
MAXS = 8
RAD = 3
LANES = 128
GROUP = 16
HALO = 16
OCTET = 8
QUAD = 4
MIB = 1 << 20


smooth_sigma = 1.0


def gauss_taps():
    positions = np.arange(-RAD, RAD + 1).astype(np.float32)
    values = np.exp(-positions * positions / np.float32(2.0 * smooth_sigma * smooth_sigma))
    return (values / values.sum(dtype=np.float32)).astype(np.float32)


def build_kernel(filters, count):
    later = jnp.arange(count)[:, None]
    earlier = jnp.arange(count)[None, :]
    offsets = later - earlier
    onehot = (offsets[:, :, None] == jnp.arange(TAPS)[None, None, :]).astype(jnp.float32)
    return jnp.sum(onehot[None] * filters[:, None, None, :], axis=-1).astype(jnp.bfloat16)


def whole_vmem(count):
    return [pl.BlockSpec(memory_space=pltpu.VMEM)] * count


def params(limit):
    return pltpu.CompilerParams(vmem_limit_bytes=limit)


def edges_kernel(place_ref, movie_ref, pair_ref, other_ref):
    frames, planes, rows, _ = movie_ref.shape
    even = place_ref[3] % 2 == 0

    def one(frame, carry):
        last = [movie_ref[frame, plane, rows - HALO :, :].astype(jnp.float32) for plane in range(planes)]
        first = [movie_ref[frame, plane, :HALO, :].astype(jnp.float32) for plane in range(planes)]
        last = [cells[OCTET:] for cells in last] + [cells[QUAD:OCTET] for cells in last]
        first = [cells[:OCTET] for cells in first] + [cells[OCTET : OCTET + QUAD] for cells in first]
        last = jnp.concatenate(last, axis=0)
        first = jnp.concatenate(first, axis=0)
        pair_ref[frame] = jnp.where(even, last, first).astype(jnp.bfloat16)
        other_ref[frame] = jnp.where(even, first, last).astype(jnp.bfloat16)
        return carry

    lax.fori_loop(0, frames, one, 0)


def edges(movie, place):
    frames, planes, _, width = movie.shape
    shape = jax.ShapeDtypeStruct((frames, planes * (OCTET + QUAD), width), jnp.bfloat16)
    return pl.pallas_call(
        edges_kernel,
        out_shape=[shape, shape],
        in_specs=[pl.BlockSpec(memory_space=pltpu.SMEM)] + whole_vmem(1),
        out_specs=whole_vmem(2),
        compiler_params=params(40 * MIB),
        name="edges",
    )(place, movie)


def pack_kernel(order, planes, place_ref, weights_ref, owner_ref, local_ref, *refs):
    *out_refs, ids = refs
    tiles = len(order)
    slots, pixels = weights_ref.shape
    octets = pixels // (planes * tiles * LANES)
    tail = planes * octets * slots
    ids[...] = jnp.zeros_like(ids)
    ids[0:1, 0:slots] = owner_ref[...].astype(jnp.float32)
    ids[1:2, 0:slots] = local_ref[...].astype(jnp.float32)
    for k, out_ref in zip(order, out_refs):
        dest = place_ref[3] ^ k
        for plane in range(planes):
            for octet in range(octets):
                lane = pl.multiple_of(((plane * tiles + dest) * octets + octet) * LANES, LANES)
                row = (plane * octets + octet) * slots
                out_ref[row : row + slots, :] = weights_ref[:, pl.ds(lane, LANES)]
        out_ref[tail:, :] = ids[...].astype(jnp.bfloat16)


def pack(weights, owner, local, order, planes, place):
    slots, pixels = weights.shape
    tiles = len(order)
    shape = jax.ShapeDtypeStruct((pixels // (tiles * LANES) * slots + GROUP, LANES), jnp.bfloat16)
    return pl.pallas_call(
        functools.partial(pack_kernel, order, planes),
        out_shape=[shape] * tiles,
        in_specs=[pl.BlockSpec(memory_space=pltpu.SMEM)] + whole_vmem(3),
        out_specs=whole_vmem(tiles),
        scratch_shapes=[pltpu.VMEM((GROUP, LANES), jnp.float32)],
        compiler_params=params(8 * MIB + 5 * weights.size),
        name="pack_weights",
    )(place, weights, owner, local)


def smooth_kernel(shift_ref, place_ref, movie_ref, other_ref, pair_ref, *refs):
    *out_refs, band, wide = refs
    frames, planes, rows, width = movie_ref.shape
    blocks = width // LANES
    reach = rows + 2 * HALO
    parts = len(out_refs)
    each = blocks // parts
    together = wide.shape[0]
    taps = gauss_taps()
    high = [float(v) for v in taps.astype(jnp.bfloat16)]
    low = [float(v) for v in taps - taps.astype(jnp.bfloat16).astype(np.float32)]
    lane = lax.broadcasted_iota(jnp.int32, (reach, LANES), 1)
    row = lax.broadcasted_iota(jnp.int32, (reach, LANES), 0)
    first_row, total_rows, me = place_ref[0], place_ref[1], place_ref[2]
    even = place_ref[3] % 2 == 0

    tap = lax.broadcasted_iota(jnp.int32, (2 * LANES, LANES), 0) - lax.broadcasted_iota(jnp.int32, (2 * LANES, LANES), 1)
    tap = tap - (MAXS - RAD)
    for side, values in enumerate((high, low)):
        cells = jnp.zeros((2 * LANES, LANES), jnp.float32)
        for i, value in enumerate(values):
            cells = jnp.where(tap == i, value, cells)
        band[:, side * LANES : (side + 1) * LANES] = cells.astype(jnp.bfloat16)

    def some(step, carry):
        chosen = [step * together + u for u in range(together)]
        stacked = []
        for frame in chosen:
            right = shift_ref[1, frame] + MAXS
            near = lane < right
            zero = jnp.zeros((reach, LANES), jnp.float32)
            for plane in range(planes):
                moved = []
                for b in range(blocks):
                    cells = slice(b * LANES, (b + 1) * LANES)
                    pair = pair_ref[frame, :, cells].astype(jnp.float32)
                    other = other_ref[frame, :, cells].astype(jnp.float32)
                    top = jnp.where(even, other, pair)
                    bottom = jnp.where(even, pair, other)
                    full = slice(plane * OCTET, (plane + 1) * OCTET)
                    rest = slice(planes * OCTET + plane * QUAD, planes * OCTET + (plane + 1) * QUAD)
                    piece = jnp.concatenate(
                        [
                            top[rest],
                            top[rest],
                            top[full],
                            movie_ref[frame, plane, :, cells].astype(jnp.float32),
                            bottom[full],
                            bottom[rest],
                            bottom[rest],
                        ],
                        axis=0,
                    )
                    moved.append(pltpu.roll(piece, right, 1))
                shifted = []
                for b in range(blocks + 1):
                    before = moved[b - 1] if b > 0 else zero
                    own = moved[b] if b < blocks else zero
                    cells = jnp.where(near, before, own)
                    if b == 0:
                        cells = jnp.where(lane < MAXS, 0.0, cells)
                    if b == blocks:
                        cells = jnp.where(lane < MAXS, cells, 0.0)
                    shifted.append(cells.astype(jnp.bfloat16))
                stacked += [jnp.concatenate(shifted[b : b + 2], axis=1) for b in range(blocks)]
        result = jnp.dot(jnp.concatenate(stacked, axis=0), band[...], preferred_element_type=jnp.float32)
        result = result[:, :LANES] + result[:, LANES:]
        for u, frame in enumerate(chosen):
            place = first_row + row - HALO + shift_ref[0, frame]
            inside = (place >= 0) & (place < total_rows)
            for plane in range(planes):
                for b in range(blocks):
                    at = ((u * planes + plane) * blocks + b) * reach
                    wide[u, plane, b] = jnp.where(inside, result[at : at + reach], 0.0)
        for u, frame in enumerate(chosen):
            start = HALO - RAD - shift_ref[0, frame]
            for plane in range(planes):
                for k in range(parts):
                    for j in range(each):
                        b = (me ^ k) * each + j
                        total = float(taps[RAD]) * wide[u, plane, b, pl.ds(start + RAD, rows), :]
                        for i in range(RAD):
                            pair = wide[u, plane, b, pl.ds(start + i, rows), :]
                            pair = pair + wide[u, plane, b, pl.ds(start + 2 * RAD - i, rows), :]
                            total = total + float(taps[i]) * pair
                        out_refs[k][frame, plane, :, j * LANES : (j + 1) * LANES] = total.astype(jnp.bfloat16)
        return carry

    lax.fori_loop(0, frames // together, some, 0)


def smooth(movie, pair, other, shifts, place, parts):
    frames, planes, rows, width = movie.shape
    reach = rows + 2 * HALO
    smem = pl.BlockSpec(memory_space=pltpu.SMEM)
    return pl.pallas_call(
        smooth_kernel,
        out_shape=[jax.ShapeDtypeStruct((frames, planes, rows, width // parts), jnp.bfloat16)] * parts,
        in_specs=[smem, smem] + whole_vmem(3),
        out_specs=whole_vmem(parts),
        scratch_shapes=[
            pltpu.VMEM((2 * LANES, 2 * LANES), jnp.bfloat16),
            pltpu.VMEM((2 - frames % 2, planes, width // LANES, reach, LANES), jnp.float32),
        ],
        compiler_params=params(20 * MIB + 8 * movie.size),
        name="smooth",
    )(shifts, place, movie, other, pair)


def spread_kernel(part_frames, place_ref, kernel_ref, out_ref):
    planes, size, _ = out_ref.shape
    frames = size // GROUP
    me = place_ref[2]
    row = lax.broadcasted_iota(jnp.int32, (size, frames), 0)
    column = lax.broadcasted_iota(jnp.int32, (size, frames), 1)
    tall = (row % frames == column).astype(jnp.bfloat16)
    row = lax.broadcasted_iota(jnp.int32, (frames, size), 0)
    column = lax.broadcasted_iota(jnp.int32, (frames, size), 1) // GROUP
    last = frames // part_frames - 1
    column = ((last - column // part_frames) ^ me) * part_frames + column % part_frames
    flat = (column == row).astype(jnp.bfloat16)
    row = lax.broadcasted_iota(jnp.int32, (size, size), 0)
    column = lax.broadcasted_iota(jnp.int32, (size, size), 1)
    same = row // frames == column % GROUP
    for plane in range(planes):
        left = jnp.dot(tall, kernel_ref[plane], preferred_element_type=jnp.float32).astype(jnp.bfloat16)
        full = jnp.dot(left, flat, preferred_element_type=jnp.float32)
        out_ref[plane] = jnp.where(same, full, 0.0).astype(jnp.bfloat16)


def spread(kernel, place, part_frames):
    planes, frames, _ = kernel.shape
    size = frames * GROUP
    return pl.pallas_call(
        functools.partial(spread_kernel, part_frames),
        out_shape=jax.ShapeDtypeStruct((planes, size, size), jnp.bfloat16),
        in_specs=[pl.BlockSpec(memory_space=pltpu.SMEM)] + whole_vmem(1),
        out_specs=whole_vmem(1)[0],
        compiler_params=params(8 * MIB + 16 * size * size),
        name="spread_filters",
    )(place, kernel)


def swap_lanes(pieces):
    count = len(pieces)
    group = LANES // count
    half = count // 2
    lane = lax.broadcasted_iota(jnp.int32, pieces[0].shape, 1) // group
    while half >= 1:
        low = (lane & half) == 0
        result = list(pieces)
        for i in range(count):
            if i & half:
                continue
            a, b = pieces[i], pieces[i + half]
            if 2 * half == count:
                back = pltpu.roll(b, half * group, 1)
                ahead = pltpu.roll(a, half * group, 1)
            else:
                back = pltpu.roll(b, half * group, 1)
                ahead = pltpu.roll(a, LANES - half * group, 1)
            result[i] = jnp.where(low, a, back)
            result[i + half] = jnp.where(low, ahead, b)
        pieces = result
        half //= 2
    return pieces


def deconvolve_kernel(parts, spread_ref, *refs):
    data_refs, out_ref = refs[:parts], refs[-1]
    part_frames, planes, rows, width = data_refs[0].shape
    size = spread_ref.shape[1]
    frames = size // GROUP
    octets = rows // OCTET
    for q in range(width // LANES):
        lanes = slice(q * LANES, (q + 1) * LANES)
        for plane in range(planes):
            for first in range(0, rows // GROUP, 2):
                cells = []
                for a in (first, first + 1):
                    pieces = [ref[:, plane, a * GROUP : (a + 1) * GROUP, lanes] for ref in data_refs]
                    cells.append(jnp.concatenate(pieces, axis=0).reshape(size, LANES))
                cells = jnp.concatenate(cells, axis=1)
                spikes = jnp.dot(spread_ref[plane], cells, preferred_element_type=jnp.float32)
                spikes = jnp.maximum(spikes, 0.0)
                for a in (0, 1):
                    for half in (0, 1):
                        pieces = [
                            spikes[(half * OCTET + r) * frames : (half * OCTET + r + 1) * frames, a * LANES : (a + 1) * LANES]
                            for r in range(OCTET)
                        ]
                        octet = plane * octets + (first + a) * 2 + half
                        for j, piece in enumerate(swap_lanes(pieces)):
                            out_ref[q, octet, j * frames : (j + 1) * frames, :] = piece.astype(jnp.bfloat16)


def deconvolve(spread_filters, data, after):
    part_frames, planes, rows, width = data[0].shape
    frames = part_frames * len(data)
    shape = (width // LANES, planes * rows // OCTET, OCTET * frames, LANES)
    return pl.pallas_call(
        functools.partial(deconvolve_kernel, len(data)),
        out_shape=jax.ShapeDtypeStruct(shape, jnp.bfloat16),
        in_specs=whole_vmem(1 + len(data)) + [pl.BlockSpec(memory_space=pl.ANY)] * len(after),
        out_specs=whole_vmem(1)[0],
        compiler_params=params(12 * MIB + 4 * (spread_filters.size + 2 * len(data) * data[0].size)),
        name="deconvolve",
    )(spread_filters, *data, *after)


def pool_kernel(order, place_ref, spikes_ref, *refs):
    *weights_refs, out_ref = refs
    blocks, steps, height, _ = spikes_ref.shape
    tiles = len(weights_refs)
    me = place_ref[3]
    near = tiles // blocks
    frames = height // near
    tail = weights_refs[0].shape[0] - GROUP
    slots = tail // steps
    owners, owner_rows, _ = out_ref.shape
    owned = owners * owner_rows
    eye = lax.broadcasted_iota(jnp.int32, (slots, LANES), 0) == lax.broadcasted_iota(jnp.int32, (slots, LANES), 1)
    keys, groups = [], []
    for ref in weights_refs:
        ids = ref[tail : tail + GROUP, :].astype(jnp.float32)
        owner = jnp.sum(jnp.where(eye, ids[0:1, :], 0.0), axis=1, keepdims=True).astype(jnp.int32)
        local = jnp.sum(jnp.where(eye, ids[1:2, :], 0.0), axis=1, keepdims=True).astype(jnp.int32)
        keys.append(owner * owner_rows + local % owner_rows)
        groups.append(local // owner_rows)
    key = jnp.concatenate(keys, axis=0)
    group = jnp.concatenate(groups, axis=0)
    onehot = (lax.broadcasted_iota(jnp.int32, (tiles * slots, owned), 1) == key).astype(jnp.bfloat16)
    total = jnp.zeros((owned, LANES), jnp.float32)
    for q in range(blocks):
        pooled = jnp.zeros((tiles * slots, height), jnp.float32)
        for step in range(0, steps, 2):
            left = jnp.concatenate(
                [
                    jnp.concatenate([ref[at * slots : (at + 1) * slots, :] for ref in weights_refs], axis=0)
                    for at in (step, step + 1)
                ],
                axis=1,
            )
            right = jnp.concatenate([spikes_ref[q, step], spikes_ref[q, step + 1]], axis=1)
            pooled = pooled + lax.dot_general(
                left, right, (((1,), (1,)), ((), ())), preferred_element_type=jnp.float32
            )
        column = lax.broadcasted_iota(jnp.int32, (slots, height), 1) // frames + q * near
        pooled = jnp.concatenate(
            [jnp.where(column == me ^ k, pooled[i * slots : (i + 1) * slots], 0.0) for i, k in enumerate(order)], axis=0
        )
        partial = pooled[:, 0:LANES]
        for at in range(LANES, height, LANES):
            partial = partial + pooled[:, at : at + LANES]
        step = LANES // 2
        while step >= frames:
            partial = partial + pltpu.roll(partial, step, 1)
            step //= 2
        lane_group = lax.broadcasted_iota(jnp.int32, partial.shape, 1) // frames
        partial = jnp.where(lane_group == group, partial, 0.0)
        high = partial.astype(jnp.bfloat16)
        low = (partial - high.astype(jnp.float32)).astype(jnp.bfloat16)
        both = lax.dot_general(
            onehot,
            jnp.concatenate([high, low], axis=1),
            (((0,), (0,)), ((), ())),
            preferred_element_type=jnp.float32,
        )
        total = total + both[:, :LANES] + both[:, LANES:]
    out_ref[...] = total.reshape(owners, owner_rows, LANES)


def pool(spikes, weights, order, place, frames, owners):
    shape = (owners, COMP_DEV * frames // LANES, LANES)
    inputs = [spikes, *weights]
    return pl.pallas_call(
        functools.partial(pool_kernel, order),
        out_shape=jax.ShapeDtypeStruct(shape, jnp.float32),
        in_specs=[pl.BlockSpec(memory_space=pltpu.SMEM)] + whole_vmem(len(inputs)),
        out_specs=whole_vmem(1)[0],
        compiler_params=params(16 * MIB + 4 * sum(cells.size for cells in inputs)),
        name="pool",
    )(place, *inputs)


def finish_kernel(parts_ref, out_ref):
    sources, rows, _ = parts_ref.shape
    frames = out_ref.shape[1]
    total = jnp.sum(parts_ref[...], axis=0)
    for group in range(LANES // frames):
        out_ref[group * rows : (group + 1) * rows, :] = total[:, group * frames : (group + 1) * frames]


def finish(parts, frames):
    return pl.pallas_call(
        finish_kernel,
        out_shape=jax.ShapeDtypeStruct((COMP_DEV, frames), jnp.float32),
        in_specs=whole_vmem(1),
        out_specs=whole_vmem(1)[0],
        compiler_params=params(8 * MIB + 8 * parts.size),
        name="finish",
    )(parts)


def body(movie, shifts, filters, weights, slot_owner, slot_local):
    part_frames, planes, rows, width = movie.shape
    tiles = lax.axis_size("tile")
    parts = lax.axis_size("frame")
    frames = part_frames * parts
    slots = weights.shape[0]
    ends = tiles - 1
    tile = lax.axis_index("tile")
    place = jnp.stack([tile * rows, tiles * rows, lax.axis_index("frame"), tile]).astype(jnp.int32)
    far, close = list(range(tiles // 2, tiles)), list(range(1, tiles // 2))
    order = close[1:2] + far[-2:] + close[:1] + far[:1] + far[-3:0:-1] + close[2:] + [0]
    owner, local = slot_owner.reshape(1, slots), slot_local.reshape(1, slots)
    pair, other = edges(movie, place)
    packed = pack(weights, owner, local, order, planes, place)
    swaps = [(i, i + 1) for i in range(1, ends, 2)]
    other = lax.ppermute(other, "tile", swaps + [(j, i) for i, j in swaps])
    pair = lax.ppermute(pair, "tile", [(i, i ^ 1) for i in range(tiles)])
    landed = [
        lax.ppermute(cells, "tile", [(i, i ^ k) for i in range(tiles)]) if k else cells
        for k, cells in zip(order, packed)
    ]
    pieces = smooth(movie, pair, other, shifts.T, place, parts)
    pieces = [
        lax.ppermute(pieces[k], "frame", [(i, i ^ k) for i in range(parts)]) for k in range(parts - 1, 0, -1)
    ] + [pieces[0]]
    spikes = deconvolve(spread(build_kernel(filters, frames), place, part_frames), pieces, landed[: len(far) + 1])
    traces = pool(spikes, landed, order, place, frames, parts * tiles)
    traces = lax.all_to_all(traces, ("frame", "tile"), split_axis=0, concat_axis=0, tiled=True)
    return finish(traces, frames)


def solution(mesh):
    in_specs = (
        P("frame", None, "tile", None),
        P("frame", None),
        P(),
        P(("frame", "tile"), None),
        P(("frame", "tile"), None),
        P(("frame", "tile"), None),
    )
    out_specs = P(("frame", "tile"), None)
    return jax.shard_map(body, mesh=mesh, in_specs=in_specs, out_specs=out_specs, check_vma=False)
```

profile of v0, /device:TPU:0, one launch (start us, length us, event | category | flops | bytes accessed | tf_op | source)
XLA Modules:
  0.0 53.6 jit_solution(9884352767084346426)
XLA Ops:
  0.1 1.2 %copy-done = bf16[8,2,64,512]{3,2,1,0:T(8,128)(2,1)S(1)} copy-done((bf16[8,2,64,512]{3,2,1,0:T(8,128)(2,1)S(1)}, bf16[8,2,64,512]{3,2,1,0:T(8,128)(2,1)}, u32[]{:S(2)}) %copy-start) | copy-done | bytes 1048600
  1.3 0.7 %edges.1 = (bf16[8,24,512]{2,1,0:T(8,128)(2,1)S(1)}, bf16[8,24,512]{2,1,0:T(8,128)(2,1)S(1)}) custom-call(s32[4]{0:T(128)S(1)} %pad_add_fusion.place_ref, bf16[8,2,64,512]{3,2,1,0:T(8,128)(2,1)S(1)} %copy-done), custom_call_target="tpu_custom_call" | custom-call | tf_op jit(solution)/shard_map/edges/pallas_call | solution.py:69
  2.0 0.7 %collective-permute-start = (bf16[8,24,512]{2,1,0:T(8,128)(2,1)S(1)}, bf16[8,24,512]{2,1,0:T(8,128)(2,1)S(1)}, u32[]{:S(2)}, u32[]{:S(2)}) collective-permute-start(bf16[8,24,512]{2,1,0:T(8,128)(2,1)S(1)} %get-tuple-element.19), channel_id=1, source_target_pairs={{1,2},{3,4},{5,6},{2,1},{4,3},{6,5},{9,10},{11,12},{13,14},{10,9},... | collective-permute-start | bytes 589832 | tf_op jit(solution)/shard_map/ppermute | solution.py:432
  2.7 5.8 %collective-permute-start.1 = (bf16[8,24,512]{2,1,0:T(8,128)(2,1)S(1)}, bf16[8,24,512]{2,1,0:T(8,128)(2,1)S(1)}, u32[]{:S(2)}, u32[]{:S(2)}) collective-permute-start(bf16[8,24,512]{2,1,0:T(8,128)(2,1)S(1)} %get-tuple-element.20), channel_id=1, source_target_pairs={{0,1},{1,0},{2,3},{3,2},{4,5},{5,4},{6,7},{7,6},{8,9},{9,8},{10,11... | collective-permute-start | bytes 589832 | tf_op jit(solution)/shard_map/ppermute | solution.py:433
  8.5 0.6 %copy-done.3 = s32[32,1]{0,1:T(1,128)S(1)} copy-done((s32[32,1]{0,1:T(1,128)S(1)}, s32[32,1]{0,1:T(1,128)}, u32[]{:S(2)}) %copy-start.3) | copy-done | bytes 152
  9.1 0.8 %pack_weights.1 = (bf16[528,128]{1,0:T(8,128)(2,1)S(1)}, bf16[528,128]{1,0:T(8,128)(2,1)S(1)}, bf16[528,128]{1,0:T(8,128)(2,1)S(1)}, bf16[528,128]{1,0:T(8,128)(...) custom-call(s32[4]{0:T(128)S(1)} %pad_add_fusion.place_ref, ...), custom_call_target="tpu_custom_call" | custom-call | tf_op jit(solution)/shard_map/pack_weights/pallas_call | solution.py:102
  9.9 1.6 %collective-permute-start.5 = (bf16[528,128]{1,0:T(8,128)(2,1)S(1)}, bf16[528,128]{1,0:T(8,128)(2,1)S(1)}, u32[]{:S(2)}, u32[]{:S(2)}) collective-permute-start(bf16[528,128]{1,0:T(8,128)(2,1)S(1)} %get-tuple-element.25), channel_id=1, source_target_pairs={{0,2},{1,3},{2,0},{3,1},{4,6},{5,7},{6,4},{7,5},{8,10},{9,11},{10,... | collective-permute-start | bytes 405512 | tf_op jit(solution)/shard_map/ppermute | solution.py:435
  11.6 2.5 %collective-permute-start.6 = (bf16[528,128]{1,0:T(8,128)(2,1)S(1)}, bf16[528,128]{1,0:T(8,128)(2,1)S(1)}, u32[]{:S(2)}, u32[]{:S(2)}) collective-permute-start(bf16[528,128]{1,0:T(8,128)(2,1)S(1)} %get-tuple-element.26), channel_id=1, source_target_pairs={{0,6},{1,7},{2,4},{3,5},{4,2},{5,3},{6,0},{7,1},{8,14},{9,15},{10,... | collective-permute-start | bytes 405512 | tf_op jit(solution)/shard_map/ppermute | solution.py:435
  14.1 1.1 %collective-permute-start.7 = (bf16[528,128]{1,0:T(8,128)(2,1)S(1)}, bf16[528,128]{1,0:T(8,128)(2,1)S(1)}, u32[]{:S(2)}, u32[]{:S(2)}) collective-permute-start(bf16[528,128]{1,0:T(8,128)(2,1)S(1)} %get-tuple-element.27), channel_id=1, source_target_pairs={{0,7},{1,6},{2,5},{3,4},{4,3},{5,2},{6,1},{7,0},{8,15},{9,14},{10,... | collective-permute-start | bytes 405512 | tf_op jit(solution)/shard_map/ppermute | solution.py:435
  15.2 1.7 %collective-permute-start.8 = (bf16[528,128]{1,0:T(8,128)(2,1)S(1)}, bf16[528,128]{1,0:T(8,128)(2,1)S(1)}, u32[]{:S(2)}, u32[]{:S(2)}) collective-permute-start(bf16[528,128]{1,0:T(8,128)(2,1)S(1)} %get-tuple-element.28), channel_id=1, source_target_pairs={{0,1},{1,0},{2,3},{3,2},{4,5},{5,4},{6,7},{7,6},{8,9},{9,8},{10,11... | collective-permute-start | bytes 405512 | tf_op jit(solution)/shard_map/ppermute | solution.py:435
  16.9 3.7 %collective-permute-start.9 = (bf16[528,128]{1,0:T(8,128)(2,1)S(1)}, bf16[528,128]{1,0:T(8,128)(2,1)S(1)}, u32[]{:S(2)}, u32[]{:S(2)}) collective-permute-start(bf16[528,128]{1,0:T(8,128)(2,1)S(1)} %get-tuple-element.29), channel_id=1, source_target_pairs={{0,4},{1,5},{2,6},{3,7},{4,0},{5,1},{6,2},{7,3},{8,12},{9,13},{10,... | collective-permute-start | bytes 405512 | tf_op jit(solution)/shard_map/ppermute | solution.py:435
  20.6 3.4 %smooth.1 = (bf16[8,2,64,128]{3,2,1,0:T(8,128)(2,1)S(1)}, bf16[8,2,64,128]{3,2,1,0:T(8,128)(2,1)S(1)}, bf16[8,2,64,128]{3,2,1,0:T(8,128)(2,1)S(1)}, bf16[8,2,64,128]{3,2,1,0:T(8,128)(2,1)S(1)}) custom-call(s32[2,8]{1,0:T(2,128)S(1)} %bitcast.6, s32[4]{0:T(128)S(1)} %pad_add_fusion.place_ref, bf16[8,2,64,512]{3,2,1,0:T(8,128)(2,1)S(1)} %copy-done, ...), custom_call_target="tpu_custom_call" | custom-call | tf_op jit(solution)/shard_map/smooth/pallas_call | solution.py:208
  24.0 0.8 %collective-permute-start.2 = (bf16[8,2,64,128]{3,2,1,0:T(8,128)(2,1)S(1)}, bf16[8,2,64,128]{3,2,1,0:T(8,128)(2,1)S(1)}, u32[]{:S(2)}, u32[]{:S(2)}) collective-permute-start(bf16[8,2,64,128]{3,2,1,0:T(8,128)(2,1)S(1)} %get-tuple-element.21), channel_id=1, source_target_pairs={{0,24},{8,16},{16,8},{24,0},{1,25},{9,17},{17,9},{25,1},{2,26},{10... | collective-permute-start | bytes 786440 | tf_op jit(solution)/shard_map/ppermute | solution.py:440
  24.8 0.8 %collective-permute-start.3 = (bf16[8,2,64,128]{3,2,1,0:T(8,128)(2,1)S(1)}, bf16[8,2,64,128]{3,2,1,0:T(8,128)(2,1)S(1)}, u32[]{:S(2)}, u32[]{:S(2)}) collective-permute-start(bf16[8,2,64,128]{3,2,1,0:T(8,128)(2,1)S(1)} %get-tuple-element.22), channel_id=1, source_target_pairs={{0,16},{8,24},{16,0},{24,8},{1,17},{9,25},{17,1},{25,9},{2,18},{10... | collective-permute-start | bytes 786440 | tf_op jit(solution)/shard_map/ppermute | solution.py:440
  25.7 0.3 collective-permute-start.4
  25.9 0.2 fusion
  26.2 5.5 %collective-permute-start.10 = (bf16[528,128]{1,0:T(8,128)(2,1)S(1)}, bf16[528,128]{1,0:T(8,128)(2,1)S(1)}, u32[]{:S(2)}, u32[]{:S(2)}) collective-permute-start(bf16[528,128]{1,0:T(8,128)(2,1)S(1)} %get-tuple-element.30), channel_id=1, source_target_pairs={{0,5},{1,4},{2,7},{3,6},{4,1},{5,0},{6,3},{7,2},{8,13},{9,12},{10,... | collective-permute-start | bytes 405512 | tf_op jit(solution)/shard_map/ppermute | solution.py:435
  31.7 0.4 multiply_reduce_fusion.kernel_ref
  32.0 1.2 %spread_filters.1.spread_ref = bf16[2,512,512]{2,1,0:T(8,128)(2,1)S(1)} custom-call(s32[4]{0:T(128)S(1)} %pad_add_fusion.place_ref, bf16[2,32,32]{2,1,0:T(8,128)(2,1)S(1)} %multiply_reduce_fusion.kernel_ref), custom_call_target="tpu_custom_call" | custom-call | tf_op jit(solution)/shard_map/spread_filters/pallas_call | solution.py:246
  33.3 5.0 %collective-permute-done.3.refs_1_ = bf16[8,2,64,128]{3,2,1,0:T(8,128)(2,1)S(1)} collective-permute-done((bf16[8,2,64,128]{3,2,1,0:T(8,128)(2,1)S(1)}, bf16[8,2,64,128]{3,2,1,0:T(8,128)(2,1)S(1)}, u32[]{:S(2)}, u32[]{:S(2)}) %collective-permute-start.3) | collective-permute-done | bytes 262176 | tf_op jit(solution)/shard_map/ppermute | solution.py:440
  38.3 1.2 %deconvolve.1.spikes_ref = bf16[1,16,256,128]{3,2,1,0:T(8,128)(2,1)S(1)} custom-call(bf16[2,512,512]{2,1,0:T(8,128)(2,1)S(1)} %spread_filters.1.spread_ref, bf16[8,2,64,128]{3,2,1,0:T(8,128)(2,1)S(1)} %collective-permute-done.2.refs_0_, bf16[8,2,64,128]{3,2,1,0:T(8,128)(2,1)S(1)} %collective-permute-done.3.refs_1_, ...), custom_call_target="tpu_custom_call" | custom-call | tf_op jit(solution)/shard_map/deconvolve/pallas_call | solution.py:313
  39.6 1.4 %pool.1 = f32[32,8,128]{2,1,0:T(8,128)S(1)} custom-call(s32[4]{0:T(128)S(1)} %pad_add_fusion.place_ref, bf16[1,16,256,128]{3,2,1,0:T(8,128)(2,1)S(1)} %deconvolve.1.spikes_ref, bf16[528,128]{1,0:T(8,128)(2,1)S(1)} %collective-permute-done.5.refs_4_.refs_0_, bf16[528,128]{1,0:T(8,128)(2,1)S(1)} %collective-permute-done.6.refs_5_.refs_1_, ...), custom_call_target="tpu_custom_call" | custom-call | tf_op jit(solution)/shard_map/pool/pallas_call | solution.py:388
  41.0 11.9 %all_to_all.5.parts_ref = f32[32,8,128]{2,1,0:T(8,128)S(1)} all-to-all(f32[32,8,128]{2,1,0:T(8,128)S(1)} %pool.1), channel_id=1, replica_groups=mesh['frame'=4,'tile'=8] {'frame','tile'}, dimensions={0} | all-to-all | bytes 262144 | tf_op jit(solution)/shard_map/all_to_all | solution.py:444
  52.9 0.7 %finish.1 = f32[32,32]{1,0:T(8,128)} custom-call(f32[32,8,128]{2,1,0:T(8,128)S(1)} %all_to_all.5.parts_ref), custom_call_target="tpu_custom_call" | custom-call | tf_op jit(solution)/shard_map/finish/pallas_call | solution.py:407
  (24 shorter events, 0.1 us)
Async XLA Ops:
  0.1 1.2 %copy-start = (bf16[8,2,64,512]{3,2,1,0:T(8,128)(2,1)S(1)}, bf16[8,2,64,512]{3,2,1,0:T(8,128)(2,1)}, u32[]{:S(2)}) copy-start(bf16[8,2,64,512]{3,2,1,0:T(8,128)(2,1)} %movie_ref.3) | copy-start | bytes 3145732
  1.3 7.1 %copy-start.1 = (bf16[32,16384]{1,0:T(8,128)(2,1)S(1)}, bf16[32,16384]{1,0:T(8,128)(2,1)}, u32[]{:S(2)}) copy-start(bf16[32,16384]{1,0:T(8,128)(2,1)} %weights_ref.1) | copy-start | bytes 3145732
  2.0 13.2 %collective-permute-start = (bf16[8,24,512]{2,1,0:T(8,128)(2,1)S(1)}, bf16[8,24,512]{2,1,0:T(8,128)(2,1)S(1)}, u32[]{:S(2)}, u32[]{:S(2)}) collective-permute-start(bf16[8,24,512]{2,1,0:T(8,128)(2,1)S(1)} %get-tuple-element.19), channel_id=1, source_target_pairs={{1,2},{3,4},{5,6},{2,1},{4,3},{6,5},{9,10},{11,12},{13,14},{10,9},... | collective-permute-start | bytes 589832 | tf_op jit(solution)/shard_map/ppermute | solution.py:432
  2.7 14.2 %collective-permute-start.1 = (bf16[8,24,512]{2,1,0:T(8,128)(2,1)S(1)}, bf16[8,24,512]{2,1,0:T(8,128)(2,1)S(1)}, u32[]{:S(2)}, u32[]{:S(2)}) collective-permute-start(bf16[8,24,512]{2,1,0:T(8,128)(2,1)S(1)} %get-tuple-element.20), channel_id=1, source_target_pairs={{0,1},{1,0},{2,3},{3,2},{4,5},{5,4},{6,7},{7,6},{8,9},{9,8},{10,11... | collective-permute-start | bytes 589832 | tf_op jit(solution)/shard_map/ppermute | solution.py:433
  8.4 0.7 %copy-start.3 = (s32[32,1]{0,1:T(1,128)S(1)}, s32[32,1]{0,1:T(1,128)}, u32[]{:S(2)}) copy-start(s32[32,1]{0,1:T(1,128)} %param.10) | copy-start | bytes 388
  8.4 0.7 %copy-start.4 = (s32[32,1]{0,1:T(1,128)S(1)}, s32[32,1]{0,1:T(1,128)}, u32[]{:S(2)}) copy-start(s32[32,1]{0,1:T(1,128)} %param.11) | copy-start | bytes 388
  9.9 14.1 %collective-permute-start.5 = (bf16[528,128]{1,0:T(8,128)(2,1)S(1)}, bf16[528,128]{1,0:T(8,128)(2,1)S(1)}, u32[]{:S(2)}, u32[]{:S(2)}) collective-permute-start(bf16[528,128]{1,0:T(8,128)(2,1)S(1)} %get-tuple-element.25), channel_id=1, source_target_pairs={{0,2},{1,3},{2,0},{3,1},{4,6},{5,7},{6,4},{7,5},{8,10},{9,11},{10,... | collective-permute-start | bytes 405512 | tf_op jit(solution)/shard_map/ppermute | solution.py:435
  11.6 13.3 %collective-permute-start.6 = (bf16[528,128]{1,0:T(8,128)(2,1)S(1)}, bf16[528,128]{1,0:T(8,128)(2,1)S(1)}, u32[]{:S(2)}, u32[]{:S(2)}) collective-permute-start(bf16[528,128]{1,0:T(8,128)(2,1)S(1)} %get-tuple-element.26), channel_id=1, source_target_pairs={{0,6},{1,7},{2,4},{3,5},{4,2},{5,3},{6,0},{7,1},{8,14},{9,15},{10,... | collective-permute-start | bytes 405512 | tf_op jit(solution)/shard_map/ppermute | solution.py:435
  14.1 11.6 %collective-permute-start.7 = (bf16[528,128]{1,0:T(8,128)(2,1)S(1)}, bf16[528,128]{1,0:T(8,128)(2,1)S(1)}, u32[]{:S(2)}, u32[]{:S(2)}) collective-permute-start(bf16[528,128]{1,0:T(8,128)(2,1)S(1)} %get-tuple-element.27), channel_id=1, source_target_pairs={{0,7},{1,6},{2,5},{3,4},{4,3},{5,2},{6,1},{7,0},{8,15},{9,14},{10,... | collective-permute-start | bytes 405512 | tf_op jit(solution)/shard_map/ppermute | solution.py:435
  15.2 10.9 %collective-permute-start.8 = (bf16[528,128]{1,0:T(8,128)(2,1)S(1)}, bf16[528,128]{1,0:T(8,128)(2,1)S(1)}, u32[]{:S(2)}, u32[]{:S(2)}) collective-permute-start(bf16[528,128]{1,0:T(8,128)(2,1)S(1)} %get-tuple-element.28), channel_id=1, source_target_pairs={{0,1},{1,0},{2,3},{3,2},{4,5},{5,4},{6,7},{7,6},{8,9},{9,8},{10,11... | collective-permute-start | bytes 405512 | tf_op jit(solution)/shard_map/ppermute | solution.py:435
  16.9 3.8 %copy-start.2 = (s32[8,2]{0,1:T(2,128)S(1)}, s32[8,2]{0,1:T(2,128)}, u32[]{:S(2)}) copy-start(s32[8,2]{0,1:T(2,128)} %param.7) | copy-start | bytes 196
  16.9 14.8 %collective-permute-start.9 = (bf16[528,128]{1,0:T(8,128)(2,1)S(1)}, bf16[528,128]{1,0:T(8,128)(2,1)S(1)}, u32[]{:S(2)}, u32[]{:S(2)}) collective-permute-start(bf16[528,128]{1,0:T(8,128)(2,1)S(1)} %get-tuple-element.29), channel_id=1, source_target_pairs={{0,4},{1,5},{2,6},{3,7},{4,0},{5,1},{6,2},{7,3},{8,12},{9,13},{10,... | collective-permute-start | bytes 405512 | tf_op jit(solution)/shard_map/ppermute | solution.py:435
  24.0 9.3 %collective-permute-start.2 = (bf16[8,2,64,128]{3,2,1,0:T(8,128)(2,1)S(1)}, bf16[8,2,64,128]{3,2,1,0:T(8,128)(2,1)S(1)}, u32[]{:S(2)}, u32[]{:S(2)}) collective-permute-start(bf16[8,2,64,128]{3,2,1,0:T(8,128)(2,1)S(1)} %get-tuple-element.21), channel_id=1, source_target_pairs={{0,24},{8,16},{16,8},{24,0},{1,25},{9,17},{17,9},{25,1},{2,26},{10... | collective-permute-start | bytes 786440 | tf_op jit(solution)/shard_map/ppermute | solution.py:440
  24.8 13.5 %collective-permute-start.3 = (bf16[8,2,64,128]{3,2,1,0:T(8,128)(2,1)S(1)}, bf16[8,2,64,128]{3,2,1,0:T(8,128)(2,1)S(1)}, u32[]{:S(2)}, u32[]{:S(2)}) collective-permute-start(bf16[8,2,64,128]{3,2,1,0:T(8,128)(2,1)S(1)} %get-tuple-element.22), channel_id=1, source_target_pairs={{0,16},{8,24},{16,0},{24,8},{1,17},{9,25},{17,1},{25,9},{2,18},{10... | collective-permute-start | bytes 786440 | tf_op jit(solution)/shard_map/ppermute | solution.py:440
  25.7 12.6 %collective-permute-start.4 = (bf16[8,2,64,128]{3,2,1,0:T(8,128)(2,1)S(1)}, bf16[8,2,64,128]{3,2,1,0:T(8,128)(2,1)S(1)}, u32[]{:S(2)}, u32[]{:S(2)}) collective-permute-start(bf16[8,2,64,128]{3,2,1,0:T(8,128)(2,1)S(1)} %get-tuple-element.23), channel_id=1, source_target_pairs={{0,8},{8,0},{16,24},{24,16},{1,9},{9,1},{17,25},{25,17},{2,10},{10... | collective-permute-start | bytes 786440 | tf_op jit(solution)/shard_map/ppermute | solution.py:440
  26.2 5.5 %copy-start.5 = (f32[2,64]{1,0:T(2,128)S(1)}, f32[2,64]{1,0:T(2,128)}, u32[]{:S(2)}) copy-start(f32[2,64]{1,0:T(2,128)} %param.8) | copy-start | bytes 1540
  26.2 13.4 %collective-permute-start.10 = (bf16[528,128]{1,0:T(8,128)(2,1)S(1)}, bf16[528,128]{1,0:T(8,128)(2,1)S(1)}, u32[]{:S(2)}, u32[]{:S(2)}) collective-permute-start(bf16[528,128]{1,0:T(8,128)(2,1)S(1)} %get-tuple-element.30), channel_id=1, source_target_pairs={{0,5},{1,4},{2,7},{3,6},{4,1},{5,0},{6,3},{7,2},{8,13},{9,12},{10,... | collective-permute-start | bytes 405512 | tf_op jit(solution)/shard_map/ppermute | solution.py:435
  31.7 7.9 %collective-permute-start.11 = (bf16[528,128]{1,0:T(8,128)(2,1)S(1)}, bf16[528,128]{1,0:T(8,128)(2,1)S(1)}, u32[]{:S(2)}, u32[]{:S(2)}) collective-permute-start(bf16[528,128]{1,0:T(8,128)(2,1)S(1)} %get-tuple-element.31), channel_id=1, source_target_pairs={{0,3},{1,2},{2,1},{3,0},{4,7},{5,6},{6,5},{7,4},{8,11},{9,10},{10,... | collective-permute-start | bytes 405512 | tf_op jit(solution)/shard_map/ppermute | solution.py:435
where the time goes:
time: 53.8 us; the launch traced here: 53.6 us
  starting transfers between devices  24.6 us (46%)
  blocking collectives  11.9 us (22%)
  Pallas kernels  9.42 us (18%)
  waiting for transfers between devices  5.05 us (9%)
  local copies, waits for them, and re-layouts  1.91 us (4%)
  other arithmetic  0.64 us (1%)
    ppermute x7, starting transfers between devices, body(): lax.ppermute(cells, 'tile', [(i, i ^ k) for i in range(tiles)])  16.2 us
    all_to_all x1, blocking collectives, body(): lax.all_to_all(traces, ('frame', 'tile'), split_axis=0, concat_axis=0, ti...  11.9 us
    ppermute x1, starting transfers between devices, body(): pair = lax.ppermute(pair, 'tile', [(i, i ^ 1) for i in range(tiles)])  5.79 us
    ppermute x3, waiting for transfers between devices, body(): lax.ppermute(pieces[k], 'frame', [(i, i ^ k) for i in range(parts)])  5.03 us
    pallas_call x1, Pallas kernels, smooth(): pl.pallas_call(smooth_kernel, out_shape=[jax.ShapeDtypeStruct((frames, pl...  3.35 us
    ppermute x3, starting transfers between devices, body(): lax.ppermute(pieces[k], 'frame', [(i, i ^ k) for i in range(parts)])  1.93 us
    unnamed x12, local copies, waits for them, and re-layouts  1.91 us
    pallas_call x1, Pallas kernels, pool(): pl.pallas_call(functools.partial(pool_kernel, order), out_shape=jax.Shape...  1.44 us
  transfers between devices with their start and end apart: 12, of which 1 were waited for; matrix products, arithmetic and copies ran while one was open for 1% of the time, Pallas kernels for 12%

commit v1 on v0

--- a/solution.py
+++ b/solution.py
@@ -424,7 +424,7 @@
     tile = lax.axis_index("tile")
     place = jnp.stack([tile * rows, tiles * rows, lax.axis_index("frame"), tile]).astype(jnp.int32)
     far, close = list(range(tiles // 2, tiles)), list(range(1, tiles // 2))
-    order = close[1:2] + far[-2:] + close[:1] + far[:1] + far[-3:0:-1] + close[2:] + [0]
+    order = close[1:2] + far[-2:] + far[:1] + close[:1] + far[-3:0:-1] + close[2:] + [0]
     owner, local = slot_owner.reshape(1, slots), slot_local.reshape(1, slots)
     pair, other = edges(movie, place)
     packed = pack(weights, owner, local, order, planes, place)

time: 53.8 us -> 53.8 us (level)
  waiting for transfers between devices: 5.05 us -> 11.2 us
  starting transfers between devices: 24.6 us -> 19.7 us
  blocking collectives: 11.9 us -> 10.6 us
    ppermute x7, waiting for transfers between devices: 0.02 us -> 10.8 us  [body(): lax.ppermute(cells, 'tile', [(i, i ^ k) for i in range(tiles)])]
    ppermute x3, waiting for transfers between devices: 5.03 us -> 0.35 us  [body(): lax.ppermute(pieces[k], 'frame', [(i, i ^ k) for i in range(parts)])]
    ppermute x7, starting transfers between devices: 16.2 us -> 11.5 us  [body(): lax.ppermute(cells, 'tile', [(i, i ^ k) for i in range(tiles)])]
    all_to_all x1, blocking collectives: 11.9 us -> 10.6 us  [body(): lax.all_to_all(traces, ('frame', 'tile'), split_axis=0, concat_axis=0, ti...]
  transfers between devices with their start and end apart: 12 -> 12, of which waited for: 1 -> 6; matrix products, arithmetic and copies ran while one was open for 1% -> 1% of each run, Pallas kernels for 12% -> 12%
where the time goes in v1:
time: 53.8 us; the launch traced here: 53.6 us
  starting transfers between devices  19.7 us (37%)
  waiting for transfers between devices  11.2 us (21%)
  blocking collectives  10.6 us (20%)
  Pallas kernels  9.41 us (17%)
  local copies, waits for them, and re-layouts  1.9 us (4%)
  other arithmetic  0.64 us (1%)
    ppermute x7, starting transfers between devices, body(): lax.ppermute(cells, 'tile', [(i, i ^ k) for i in range(tiles)])  11.5 us
    ppermute x7, waiting for transfers between devices, body(): lax.ppermute(cells, 'tile', [(i, i ^ k) for i in range(tiles)])  10.8 us
    all_to_all x1, blocking collectives, body(): lax.all_to_all(traces, ('frame', 'tile'), split_axis=0, concat_axis=0, ti...  10.6 us
    ppermute x1, starting transfers between devices, body(): pair = lax.ppermute(pair, 'tile', [(i, i ^ 1) for i in range(tiles)])  5.79 us
    pallas_call x1, Pallas kernels, smooth(): pl.pallas_call(smooth_kernel, out_shape=[jax.ShapeDtypeStruct((frames, pl...  3.35 us
    unnamed x12, local copies, waits for them, and re-layouts  1.9 us
    ppermute x3, starting transfers between devices, body(): lax.ppermute(pieces[k], 'frame', [(i, i ^ k) for i in range(parts)])  1.78 us
    pallas_call x1, Pallas kernels, pool(): pl.pallas_call(functools.partial(pool_kernel, order), out_shape=jax.Shape...  1.44 us
  transfers between devices with their start and end apart: 12, of which 6 were waited for; matrix products, arithmetic and copies ran while one was open for 1% of the time, Pallas kernels for 12%

profile of v1, /device:TPU:0, one launch (start us, length us, event | category | flops | bytes accessed | tf_op | source)
XLA Modules:
  0.0 53.6 jit_solution(5145961689670987356)
XLA Ops:
  0.1 1.2 %copy-done = bf16[8,2,64,512]{3,2,1,0:T(8,128)(2,1)S(1)} copy-done((bf16[8,2,64,512]{3,2,1,0:T(8,128)(2,1)S(1)}, bf16[8,2,64,512]{3,2,1,0:T(8,128)(2,1)}, u32[]{:S(2)}) %copy-start) | copy-done | bytes 1048600
  1.3 0.7 %edges.1 = (bf16[8,24,512]{2,1,0:T(8,128)(2,1)S(1)}, bf16[8,24,512]{2,1,0:T(8,128)(2,1)S(1)}) custom-call(s32[4]{0:T(128)S(1)} %pad_add_fusion.place_ref, bf16[8,2,64,512]{3,2,1,0:T(8,128)(2,1)S(1)} %copy-done), custom_call_target="tpu_custom_call" | custom-call | tf_op jit(solution)/shard_map/edges/pallas_call | solution.py:69
  2.0 0.7 %collective-permute-start = (bf16[8,24,512]{2,1,0:T(8,128)(2,1)S(1)}, bf16[8,24,512]{2,1,0:T(8,128)(2,1)S(1)}, u32[]{:S(2)}, u32[]{:S(2)}) collective-permute-start(bf16[8,24,512]{2,1,0:T(8,128)(2,1)S(1)} %get-tuple-element.19), channel_id=1, source_target_pairs={{1,2},{3,4},{5,6},{2,1},{4,3},{6,5},{9,10},{11,12},{13,14},{10,9},... | collective-permute-start | bytes 589832 | tf_op jit(solution)/shard_map/ppermute | solution.py:432
  2.7 5.8 %collective-permute-start.1 = (bf16[8,24,512]{2,1,0:T(8,128)(2,1)S(1)}, bf16[8,24,512]{2,1,0:T(8,128)(2,1)S(1)}, u32[]{:S(2)}, u32[]{:S(2)}) collective-permute-start(bf16[8,24,512]{2,1,0:T(8,128)(2,1)S(1)} %get-tuple-element.20), channel_id=1, source_target_pairs={{0,1},{1,0},{2,3},{3,2},{4,5},{5,4},{6,7},{7,6},{8,9},{9,8},{10,11... | collective-permute-start | bytes 589832 | tf_op jit(solution)/shard_map/ppermute | solution.py:433
  8.5 0.6 %copy-done.3 = s32[32,1]{0,1:T(1,128)S(1)} copy-done((s32[32,1]{0,1:T(1,128)S(1)}, s32[32,1]{0,1:T(1,128)}, u32[]{:S(2)}) %copy-start.3) | copy-done | bytes 152
  9.1 0.8 %pack_weights.1 = (bf16[528,128]{1,0:T(8,128)(2,1)S(1)}, bf16[528,128]{1,0:T(8,128)(2,1)S(1)}, bf16[528,128]{1,0:T(8,128)(2,1)S(1)}, bf16[528,128]{1,0:T(8,128)(...) custom-call(s32[4]{0:T(128)S(1)} %pad_add_fusion.place_ref, ...), custom_call_target="tpu_custom_call" | custom-call | tf_op jit(solution)/shard_map/pack_weights/pallas_call | solution.py:102
  9.9 1.6 %collective-permute-start.5 = (bf16[528,128]{1,0:T(8,128)(2,1)S(1)}, bf16[528,128]{1,0:T(8,128)(2,1)S(1)}, u32[]{:S(2)}, u32[]{:S(2)}) collective-permute-start(bf16[528,128]{1,0:T(8,128)(2,1)S(1)} %get-tuple-element.25), channel_id=1, source_target_pairs={{0,2},{1,3},{2,0},{3,1},{4,6},{5,7},{6,4},{7,5},{8,10},{9,11},{10,... | collective-permute-start | bytes 405512 | tf_op jit(solution)/shard_map/ppermute | solution.py:435
  11.6 2.5 %collective-permute-start.6 = (bf16[528,128]{1,0:T(8,128)(2,1)S(1)}, bf16[528,128]{1,0:T(8,128)(2,1)S(1)}, u32[]{:S(2)}, u32[]{:S(2)}) collective-permute-start(bf16[528,128]{1,0:T(8,128)(2,1)S(1)} %get-tuple-element.26), channel_id=1, source_target_pairs={{0,6},{1,7},{2,4},{3,5},{4,2},{5,3},{6,0},{7,1},{8,14},{9,15},{10,... | collective-permute-start | bytes 405512 | tf_op jit(solution)/shard_map/ppermute | solution.py:435
  14.1 1.1 %collective-permute-start.7 = (bf16[528,128]{1,0:T(8,128)(2,1)S(1)}, bf16[528,128]{1,0:T(8,128)(2,1)S(1)}, u32[]{:S(2)}, u32[]{:S(2)}) collective-permute-start(bf16[528,128]{1,0:T(8,128)(2,1)S(1)} %get-tuple-element.27), channel_id=1, source_target_pairs={{0,7},{1,6},{2,5},{3,4},{4,3},{5,2},{6,1},{7,0},{8,15},{9,14},{10,... | collective-permute-start | bytes 405512 | tf_op jit(solution)/shard_map/ppermute | solution.py:435
  15.2 0.8 %collective-permute-start.8 = (bf16[528,128]{1,0:T(8,128)(2,1)S(1)}, bf16[528,128]{1,0:T(8,128)(2,1)S(1)}, u32[]{:S(2)}, u32[]{:S(2)}) collective-permute-start(bf16[528,128]{1,0:T(8,128)(2,1)S(1)} %get-tuple-element.28), channel_id=1, source_target_pairs={{0,4},{1,5},{2,6},{3,7},{4,0},{5,1},{6,2},{7,3},{8,12},{9,13},{10,... | collective-permute-start | bytes 405512 | tf_op jit(solution)/shard_map/ppermute | solution.py:435
  16.1 2.5 %collective-permute-start.9 = (bf16[528,128]{1,0:T(8,128)(2,1)S(1)}, bf16[528,128]{1,0:T(8,128)(2,1)S(1)}, u32[]{:S(2)}, u32[]{:S(2)}) collective-permute-start(bf16[528,128]{1,0:T(8,128)(2,1)S(1)} %get-tuple-element.29), channel_id=1, source_target_pairs={{0,1},{1,0},{2,3},{3,2},{4,5},{5,4},{6,7},{7,6},{8,9},{9,8},{10,11... | collective-permute-start | bytes 405512 | tf_op jit(solution)/shard_map/ppermute | solution.py:435
  18.6 3.3 %smooth.1 = (bf16[8,2,64,128]{3,2,1,0:T(8,128)(2,1)S(1)}, bf16[8,2,64,128]{3,2,1,0:T(8,128)(2,1)S(1)}, bf16[8,2,64,128]{3,2,1,0:T(8,128)(2,1)S(1)}, bf16[8,2,64,128]{3,2,1,0:T(8,128)(2,1)S(1)}) custom-call(s32[2,8]{1,0:T(2,128)S(1)} %bitcast.6, s32[4]{0:T(128)S(1)} %pad_add_fusion.place_ref, bf16[8,2,64,512]{3,2,1,0:T(8,128)(2,1)S(1)} %copy-done, ...), custom_call_target="tpu_custom_call" | custom-call | tf_op jit(solution)/shard_map/smooth/pallas_call | solution.py:208
  21.9 0.9 %collective-permute-start.2 = (bf16[8,2,64,128]{3,2,1,0:T(8,128)(2,1)S(1)}, bf16[8,2,64,128]{3,2,1,0:T(8,128)(2,1)S(1)}, u32[]{:S(2)}, u32[]{:S(2)}) collective-permute-start(bf16[8,2,64,128]{3,2,1,0:T(8,128)(2,1)S(1)} %get-tuple-element.21), channel_id=1, source_target_pairs={{0,24},{8,16},{16,8},{24,0},{1,25},{9,17},{17,9},{25,1},{2,26},{10... | collective-permute-start | bytes 786440 | tf_op jit(solution)/shard_map/ppermute | solution.py:440
  22.9 0.7 %collective-permute-start.3 = (bf16[8,2,64,128]{3,2,1,0:T(8,128)(2,1)S(1)}, bf16[8,2,64,128]{3,2,1,0:T(8,128)(2,1)S(1)}, u32[]{:S(2)}, u32[]{:S(2)}) collective-permute-start(bf16[8,2,64,128]{3,2,1,0:T(8,128)(2,1)S(1)} %get-tuple-element.22), channel_id=1, source_target_pairs={{0,16},{8,24},{16,0},{24,8},{1,17},{9,25},{17,1},{25,9},{2,18},{10... | collective-permute-start | bytes 786440 | tf_op jit(solution)/shard_map/ppermute | solution.py:440
  24.1 7.2 %collective-permute-done.8.refs_7_.refs_3_ = bf16[528,128]{1,0:T(8,128)(2,1)S(1)} collective-permute-done((bf16[528,128]{1,0:T(8,128)(2,1)S(1)}, bf16[528,128]{1,0:T(8,128)(2,1)S(1)}, u32[]{:S(2)}, u32[]{:S(2)}) %collective-permute-start.8) | collective-permute-done | bytes 135200 | tf_op jit(solution)/shard_map/ppermute | solution.py:435
  31.3 0.3 collective-permute-start.10
  31.7 2.6 %collective-permute-start.11 = (bf16[528,128]{1,0:T(8,128)(2,1)S(1)}, bf16[528,128]{1,0:T(8,128)(2,1)S(1)}, u32[]{:S(2)}, u32[]{:S(2)}) collective-permute-start(bf16[528,128]{1,0:T(8,128)(2,1)S(1)} %get-tuple-element.31), channel_id=1, source_target_pairs={{0,3},{1,2},{2,1},{3,0},{4,7},{5,6},{6,5},{7,4},{8,11},{9,10},{10,... | collective-permute-start | bytes 405512 | tf_op jit(solution)/shard_map/ppermute | solution.py:435
  34.3 0.4 multiply_reduce_fusion.kernel_ref
  34.6 1.2 %spread_filters.1.spread_ref = bf16[2,512,512]{2,1,0:T(8,128)(2,1)S(1)} custom-call(s32[4]{0:T(128)S(1)} %pad_add_fusion.place_ref, bf16[2,32,32]{2,1,0:T(8,128)(2,1)S(1)} %multiply_reduce_fusion.kernel_ref), custom_call_target="tpu_custom_call" | custom-call | tf_op jit(solution)/shard_map/spread_filters/pallas_call | solution.py:246
  36.2 1.2 %deconvolve.1.spikes_ref = bf16[1,16,256,128]{3,2,1,0:T(8,128)(2,1)S(1)} custom-call(bf16[2,512,512]{2,1,0:T(8,128)(2,1)S(1)} %spread_filters.1.spread_ref, bf16[8,2,64,128]{3,2,1,0:T(8,128)(2,1)S(1)} %collective-permute-done.2.refs_0_, bf16[8,2,64,128]{3,2,1,0:T(8,128)(2,1)S(1)} %collective-permute-done.3.refs_1_, ...), custom_call_target="tpu_custom_call" | custom-call | tf_op jit(solution)/shard_map/deconvolve/pallas_call | solution.py:313
  37.5 3.1 %collective-permute-done.10.refs_5_ = bf16[528,128]{1,0:T(8,128)(2,1)S(1)} collective-permute-done((bf16[528,128]{1,0:T(8,128)(2,1)S(1)}, bf16[528,128]{1,0:T(8,128)(2,1)S(1)}, u32[]{:S(2)}, u32[]{:S(2)}) %collective-permute-start.10) | collective-permute-done | bytes 135200 | tf_op jit(solution)/shard_map/ppermute | solution.py:435
  40.8 1.4 %pool.1 = f32[32,8,128]{2,1,0:T(8,128)S(1)} custom-call(s32[4]{0:T(128)S(1)} %pad_add_fusion.place_ref, bf16[1,16,256,128]{3,2,1,0:T(8,128)(2,1)S(1)} %deconvolve.1.spikes_ref, bf16[528,128]{1,0:T(8,128)(2,1)S(1)} %collective-permute-done.5.refs_4_.refs_0_, bf16[528,128]{1,0:T(8,128)(2,1)S(1)} %collective-permute-done.6.refs_5_.refs_1_, ...), custom_call_target="tpu_custom_call" | custom-call | tf_op jit(solution)/shard_map/pool/pallas_call | solution.py:388
  42.3 10.6 %all_to_all.5.parts_ref = f32[32,8,128]{2,1,0:T(8,128)S(1)} all-to-all(f32[32,8,128]{2,1,0:T(8,128)S(1)} %pool.1), channel_id=1, replica_groups=mesh['frame'=4,'tile'=8] {'frame','tile'}, dimensions={0} | all-to-all | bytes 262144 | tf_op jit(solution)/shard_map/all_to_all | solution.py:444
  52.9 0.7 %finish.1 = f32[32,32]{1,0:T(8,128)} custom-call(f32[32,8,128]{2,1,0:T(8,128)S(1)} %all_to_all.5.parts_ref), custom_call_target="tpu_custom_call" | custom-call | tf_op jit(solution)/shard_map/finish/pallas_call | solution.py:407
  (24 shorter events, 1.2 us)
Async XLA Ops:
  0.1 1.2 %copy-start = (bf16[8,2,64,512]{3,2,1,0:T(8,128)(2,1)S(1)}, bf16[8,2,64,512]{3,2,1,0:T(8,128)(2,1)}, u32[]{:S(2)}) copy-start(bf16[8,2,64,512]{3,2,1,0:T(8,128)(2,1)} %movie_ref.3) | copy-start | bytes 3145732
  1.3 7.1 %copy-start.1 = (bf16[32,16384]{1,0:T(8,128)(2,1)S(1)}, bf16[32,16384]{1,0:T(8,128)(2,1)}, u32[]{:S(2)}) copy-start(bf16[32,16384]{1,0:T(8,128)(2,1)} %weights_ref.1) | copy-start | bytes 3145732
  2.0 13.2 %collective-permute-start = (bf16[8,24,512]{2,1,0:T(8,128)(2,1)S(1)}, bf16[8,24,512]{2,1,0:T(8,128)(2,1)S(1)}, u32[]{:S(2)}, u32[]{:S(2)}) collective-permute-start(bf16[8,24,512]{2,1,0:T(8,128)(2,1)S(1)} %get-tuple-element.19), channel_id=1, source_target_pairs={{1,2},{3,4},{5,6},{2,1},{4,3},{6,5},{9,10},{11,12},{13,14},{10,9},... | collective-permute-start | bytes 589832 | tf_op jit(solution)/shard_map/ppermute | solution.py:432
  2.7 13.4 %collective-permute-start.1 = (bf16[8,24,512]{2,1,0:T(8,128)(2,1)S(1)}, bf16[8,24,512]{2,1,0:T(8,128)(2,1)S(1)}, u32[]{:S(2)}, u32[]{:S(2)}) collective-permute-start(bf16[8,24,512]{2,1,0:T(8,128)(2,1)S(1)} %get-tuple-element.20), channel_id=1, source_target_pairs={{0,1},{1,0},{2,3},{3,2},{4,5},{5,4},{6,7},{7,6},{8,9},{9,8},{10,11... | collective-permute-start | bytes 589832 | tf_op jit(solution)/shard_map/ppermute | solution.py:433
  8.4 0.7 %copy-start.3 = (s32[32,1]{0,1:T(1,128)S(1)}, s32[32,1]{0,1:T(1,128)}, u32[]{:S(2)}) copy-start(s32[32,1]{0,1:T(1,128)} %param.10) | copy-start | bytes 388
  8.4 0.7 %copy-start.4 = (s32[32,1]{0,1:T(1,128)S(1)}, s32[32,1]{0,1:T(1,128)}, u32[]{:S(2)}) copy-start(s32[32,1]{0,1:T(1,128)} %param.11) | copy-start | bytes 388
  9.9 12.0 %collective-permute-start.5 = (bf16[528,128]{1,0:T(8,128)(2,1)S(1)}, bf16[528,128]{1,0:T(8,128)(2,1)S(1)}, u32[]{:S(2)}, u32[]{:S(2)}) collective-permute-start(bf16[528,128]{1,0:T(8,128)(2,1)S(1)} %get-tuple-element.25), channel_id=1, source_target_pairs={{0,2},{1,3},{2,0},{3,1},{4,6},{5,7},{6,4},{7,5},{8,10},{9,11},{10,... | collective-permute-start | bytes 405512 | tf_op jit(solution)/shard_map/ppermute | solution.py:435
  11.6 11.3 %collective-permute-start.6 = (bf16[528,128]{1,0:T(8,128)(2,1)S(1)}, bf16[528,128]{1,0:T(8,128)(2,1)S(1)}, u32[]{:S(2)}, u32[]{:S(2)}) collective-permute-start(bf16[528,128]{1,0:T(8,128)(2,1)S(1)} %get-tuple-element.26), channel_id=1, source_target_pairs={{0,6},{1,7},{2,4},{3,5},{4,2},{5,3},{6,0},{7,1},{8,14},{9,15},{10,... | collective-permute-start | bytes 405512 | tf_op jit(solution)/shard_map/ppermute | solution.py:435
  14.1 9.7 %collective-permute-start.7 = (bf16[528,128]{1,0:T(8,128)(2,1)S(1)}, bf16[528,128]{1,0:T(8,128)(2,1)S(1)}, u32[]{:S(2)}, u32[]{:S(2)}) collective-permute-start(bf16[528,128]{1,0:T(8,128)(2,1)S(1)} %get-tuple-element.27), channel_id=1, source_target_pairs={{0,7},{1,6},{2,5},{3,4},{4,3},{5,2},{6,1},{7,0},{8,15},{9,14},{10,... | collective-permute-start | bytes 405512 | tf_op jit(solution)/shard_map/ppermute | solution.py:435
  15.2 16.1 %collective-permute-start.8 = (bf16[528,128]{1,0:T(8,128)(2,1)S(1)}, bf16[528,128]{1,0:T(8,128)(2,1)S(1)}, u32[]{:S(2)}, u32[]{:S(2)}) collective-permute-start(bf16[528,128]{1,0:T(8,128)(2,1)S(1)} %get-tuple-element.28), channel_id=1, source_target_pairs={{0,4},{1,5},{2,6},{3,7},{4,0},{5,1},{6,2},{7,3},{8,12},{9,13},{10,... | collective-permute-start | bytes 405512 | tf_op jit(solution)/shard_map/ppermute | solution.py:435
  16.1 2.5 %copy-start.2 = (s32[8,2]{0,1:T(2,128)S(1)}, s32[8,2]{0,1:T(2,128)}, u32[]{:S(2)}) copy-start(s32[8,2]{0,1:T(2,128)} %param.7) | copy-start | bytes 196
  16.1 15.6 %collective-permute-start.9 = (bf16[528,128]{1,0:T(8,128)(2,1)S(1)}, bf16[528,128]{1,0:T(8,128)(2,1)S(1)}, u32[]{:S(2)}, u32[]{:S(2)}) collective-permute-start(bf16[528,128]{1,0:T(8,128)(2,1)S(1)} %get-tuple-element.29), channel_id=1, source_target_pairs={{0,1},{1,0},{2,3},{3,2},{4,5},{5,4},{6,7},{7,6},{8,9},{9,8},{10,11... | collective-permute-start | bytes 405512 | tf_op jit(solution)/shard_map/ppermute | solution.py:435
  21.9 13.9 %collective-permute-start.2 = (bf16[8,2,64,128]{3,2,1,0:T(8,128)(2,1)S(1)}, bf16[8,2,64,128]{3,2,1,0:T(8,128)(2,1)S(1)}, u32[]{:S(2)}, u32[]{:S(2)}) collective-permute-start(bf16[8,2,64,128]{3,2,1,0:T(8,128)(2,1)S(1)} %get-tuple-element.21), channel_id=1, source_target_pairs={{0,24},{8,16},{16,8},{24,0},{1,25},{9,17},{17,9},{25,1},{2,26},{10... | collective-permute-start | bytes 786440 | tf_op jit(solution)/shard_map/ppermute | solution.py:440
  22.9 13.4 %collective-permute-start.3 = (bf16[8,2,64,128]{3,2,1,0:T(8,128)(2,1)S(1)}, bf16[8,2,64,128]{3,2,1,0:T(8,128)(2,1)S(1)}, u32[]{:S(2)}, u32[]{:S(2)}) collective-permute-start(bf16[8,2,64,128]{3,2,1,0:T(8,128)(2,1)S(1)} %get-tuple-element.22), channel_id=1, source_target_pairs={{0,16},{8,24},{16,0},{24,8},{1,17},{9,25},{17,1},{25,9},{2,18},{10... | collective-permute-start | bytes 786440 | tf_op jit(solution)/shard_map/ppermute | solution.py:440
  23.8 12.5 %collective-permute-start.4 = (bf16[8,2,64,128]{3,2,1,0:T(8,128)(2,1)S(1)}, bf16[8,2,64,128]{3,2,1,0:T(8,128)(2,1)S(1)}, u32[]{:S(2)}, u32[]{:S(2)}) collective-permute-start(bf16[8,2,64,128]{3,2,1,0:T(8,128)(2,1)S(1)} %get-tuple-element.23), channel_id=1, source_target_pairs={{0,8},{8,0},{16,24},{24,16},{1,9},{9,1},{17,25},{25,17},{2,10},{10... | collective-permute-start | bytes 786440 | tf_op jit(solution)/shard_map/ppermute | solution.py:440
  31.3 3.0 %copy-start.5 = (f32[2,64]{1,0:T(2,128)S(1)}, f32[2,64]{1,0:T(2,128)}, u32[]{:S(2)}) copy-start(f32[2,64]{1,0:T(2,128)} %param.8) | copy-start | bytes 1540
  31.3 9.2 %collective-permute-start.10 = (bf16[528,128]{1,0:T(8,128)(2,1)S(1)}, bf16[528,128]{1,0:T(8,128)(2,1)S(1)}, u32[]{:S(2)}, u32[]{:S(2)}) collective-permute-start(bf16[528,128]{1,0:T(8,128)(2,1)S(1)} %get-tuple-element.30), channel_id=1, source_target_pairs={{0,5},{1,4},{2,7},{3,6},{4,1},{5,0},{6,3},{7,2},{8,13},{9,12},{10,... | collective-permute-start | bytes 405512 | tf_op jit(solution)/shard_map/ppermute | solution.py:435
  31.7 9.1 %collective-permute-start.11 = (bf16[528,128]{1,0:T(8,128)(2,1)S(1)}, bf16[528,128]{1,0:T(8,128)(2,1)S(1)}, u32[]{:S(2)}, u32[]{:S(2)}) collective-permute-start(bf16[528,128]{1,0:T(8,128)(2,1)S(1)} %get-tuple-element.31), channel_id=1, source_target_pairs={{0,3},{1,2},{2,1},{3,0},{4,7},{5,6},{6,5},{7,4},{8,11},{9,10},{10,... | collective-permute-start | bytes 405512 | tf_op jit(solution)/shard_map/ppermute | solution.py:435

commit v2 on v1

--- a/solution.py
+++ b/solution.py
@@ -424,7 +424,7 @@
     tile = lax.axis_index("tile")
     place = jnp.stack([tile * rows, tiles * rows, lax.axis_index("frame"), tile]).astype(jnp.int32)
     far, close = list(range(tiles // 2, tiles)), list(range(1, tiles // 2))
-    order = close[1:2] + far[-2:] + far[:1] + close[:1] + far[-3:0:-1] + close[2:] + [0]
+    order = close[1:2] + far[-2:-1] + far[:1] + close[:1] + far[-1:] + far[-3:0:-1] + close[2:] + [0]
     owner, local = slot_owner.reshape(1, slots), slot_local.reshape(1, slots)
     pair, other = edges(movie, place)
     packed = pack(weights, owner, local, order, planes, place)

time: 53.8 us -> 53.8 us (level)
  waiting for transfers between devices: 11.2 us -> 9.79 us
  starting transfers between devices: 19.7 us -> 20.6 us
    ppermute x7, waiting for transfers between devices: 10.8 us -> 6.23 us  [body(): lax.ppermute(cells, 'tile', [(i, i ^ k) for i in range(tiles)])]
    ppermute x3, waiting for transfers between devices: 0.35 us -> 2.77 us  [body(): lax.ppermute(pieces[k], 'frame', [(i, i ^ k) for i in range(parts)])]
    ppermute x7, starting transfers between devices: 11.5 us -> 12.5 us  [body(): lax.ppermute(cells, 'tile', [(i, i ^ k) for i in range(tiles)])]
    ppermute x1, waiting for transfers between devices: 0.07 us -> 0.79 us  [body(): pair = lax.ppermute(pair, 'tile', [(i, i ^ 1) for i in range(tiles)])]
  transfers between devices with their start and end apart: 12 -> 12, of which waited for: 6 -> 5; matrix products, arithmetic and copies ran while one was open for 1% -> 1% of each run, Pallas kernels for 12% -> 12%
where the time goes in v2:
time: 53.8 us; the launch traced here: 53.6 us
  starting transfers between devices  20.6 us (38%)
  blocking collectives  11.1 us (21%)
  waiting for transfers between devices  9.79 us (18%)
  Pallas kernels  9.41 us (17%)
  local copies, waits for them, and re-layouts  1.91 us (4%)
  other arithmetic  0.64 us (1%)
    ppermute x7, starting transfers between devices, body(): lax.ppermute(cells, 'tile', [(i, i ^ k) for i in range(tiles)])  12.5 us
    all_to_all x1, blocking collectives, body(): lax.all_to_all(traces, ('frame', 'tile'), split_axis=0, concat_axis=0, ti...  11.1 us
    ppermute x7, waiting for transfers between devices, body(): lax.ppermute(cells, 'tile', [(i, i ^ k) for i in range(tiles)])  6.23 us
    ppermute x1, starting transfers between devices, body(): pair = lax.ppermute(pair, 'tile', [(i, i ^ 1) for i in range(tiles)])  5.79 us
    pallas_call x1, Pallas kernels, smooth(): pl.pallas_call(smooth_kernel, out_shape=[jax.ShapeDtypeStruct((frames, pl...  3.35 us
    ppermute x3, waiting for transfers between devices, body(): lax.ppermute(pieces[k], 'frame', [(i, i ^ k) for i in range(parts)])  2.77 us
    unnamed x12, local copies, waits for them, and re-layouts  1.91 us
    ppermute x3, starting transfers between devices, body(): lax.ppermute(pieces[k], 'frame', [(i, i ^ k) for i in range(parts)])  1.67 us
  transfers between devices with their start and end apart: 12, of which 5 were waited for; matrix products, arithmetic and copies ran while one was open for 1% of the time, Pallas kernels for 12%

profile of v2, /device:TPU:0, one launch (start us, length us, event | category | flops | bytes accessed | tf_op | source)
XLA Modules:
  0.0 53.6 jit_solution(10375523763892745685)
XLA Ops:
  0.1 1.2 %copy-done = bf16[8,2,64,512]{3,2,1,0:T(8,128)(2,1)S(1)} copy-done((bf16[8,2,64,512]{3,2,1,0:T(8,128)(2,1)S(1)}, bf16[8,2,64,512]{3,2,1,0:T(8,128)(2,1)}, u32[]{:S(2)}) %copy-start) | copy-done | bytes 1048600
  1.3 0.7 %edges.1 = (bf16[8,24,512]{2,1,0:T(8,128)(2,1)S(1)}, bf16[8,24,512]{2,1,0:T(8,128)(2,1)S(1)}) custom-call(s32[4]{0:T(128)S(1)} %pad_add_fusion.place_ref, bf16[8,2,64,512]{3,2,1,0:T(8,128)(2,1)S(1)} %copy-done), custom_call_target="tpu_custom_call" | custom-call | tf_op jit(solution)/shard_map/edges/pallas_call | solution.py:69
  2.0 0.7 %collective-permute-start = (bf16[8,24,512]{2,1,0:T(8,128)(2,1)S(1)}, bf16[8,24,512]{2,1,0:T(8,128)(2,1)S(1)}, u32[]{:S(2)}, u32[]{:S(2)}) collective-permute-start(bf16[8,24,512]{2,1,0:T(8,128)(2,1)S(1)} %get-tuple-element.19), channel_id=1, source_target_pairs={{1,2},{3,4},{5,6},{2,1},{4,3},{6,5},{9,10},{11,12},{13,14},{10,9},... | collective-permute-start | bytes 589832 | tf_op jit(solution)/shard_map/ppermute | solution.py:432
  2.7 5.8 %collective-permute-start.1 = (bf16[8,24,512]{2,1,0:T(8,128)(2,1)S(1)}, bf16[8,24,512]{2,1,0:T(8,128)(2,1)S(1)}, u32[]{:S(2)}, u32[]{:S(2)}) collective-permute-start(bf16[8,24,512]{2,1,0:T(8,128)(2,1)S(1)} %get-tuple-element.20), channel_id=1, source_target_pairs={{0,1},{1,0},{2,3},{3,2},{4,5},{5,4},{6,7},{7,6},{8,9},{9,8},{10,11... | collective-permute-start | bytes 589832 | tf_op jit(solution)/shard_map/ppermute | solution.py:433
  8.5 0.6 %copy-done.3 = s32[32,1]{0,1:T(1,128)S(1)} copy-done((s32[32,1]{0,1:T(1,128)S(1)}, s32[32,1]{0,1:T(1,128)}, u32[]{:S(2)}) %copy-start.3) | copy-done | bytes 152
  9.1 0.8 %pack_weights.1 = (bf16[528,128]{1,0:T(8,128)(2,1)S(1)}, bf16[528,128]{1,0:T(8,128)(2,1)S(1)}, bf16[528,128]{1,0:T(8,128)(2,1)S(1)}, bf16[528,128]{1,0:T(8,128)(...) custom-call(s32[4]{0:T(128)S(1)} %pad_add_fusion.place_ref, ...), custom_call_target="tpu_custom_call" | custom-call | tf_op jit(solution)/shard_map/pack_weights/pallas_call | solution.py:102
  9.9 1.6 %collective-permute-start.5 = (bf16[528,128]{1,0:T(8,128)(2,1)S(1)}, bf16[528,128]{1,0:T(8,128)(2,1)S(1)}, u32[]{:S(2)}, u32[]{:S(2)}) collective-permute-start(bf16[528,128]{1,0:T(8,128)(2,1)S(1)} %get-tuple-element.25), channel_id=1, source_target_pairs={{0,2},{1,3},{2,0},{3,1},{4,6},{5,7},{6,4},{7,5},{8,10},{9,11},{10,... | collective-permute-start | bytes 405512 | tf_op jit(solution)/shard_map/ppermute | solution.py:435
  11.6 2.5 %collective-permute-start.6 = (bf16[528,128]{1,0:T(8,128)(2,1)S(1)}, bf16[528,128]{1,0:T(8,128)(2,1)S(1)}, u32[]{:S(2)}, u32[]{:S(2)}) collective-permute-start(bf16[528,128]{1,0:T(8,128)(2,1)S(1)} %get-tuple-element.26), channel_id=1, source_target_pairs={{0,6},{1,7},{2,4},{3,5},{4,2},{5,3},{6,0},{7,1},{8,14},{9,15},{10,... | collective-permute-start | bytes 405512 | tf_op jit(solution)/shard_map/ppermute | solution.py:435
  14.1 1.3 %collective-permute-start.8 = (bf16[528,128]{1,0:T(8,128)(2,1)S(1)}, bf16[528,128]{1,0:T(8,128)(2,1)S(1)}, u32[]{:S(2)}, u32[]{:S(2)}) collective-permute-start(bf16[528,128]{1,0:T(8,128)(2,1)S(1)} %get-tuple-element.28), channel_id=1, source_target_pairs={{0,1},{1,0},{2,3},{3,2},{4,5},{5,4},{6,7},{7,6},{8,9},{9,8},{10,11... | collective-permute-start | bytes 405512 | tf_op jit(solution)/shard_map/ppermute | solution.py:435
  15.4 0.8 %collective-permute-done.1.pair_ref = bf16[8,24,512]{2,1,0:T(8,128)(2,1)S(1)} collective-permute-done((bf16[8,24,512]{2,1,0:T(8,128)(2,1)S(1)}, bf16[8,24,512]{2,1,0:T(8,128)(2,1)S(1)}, u32[]{:S(2)}, u32[]{:S(2)}) %collective-permute-start.1) | collective-permute-done | bytes 196640 | tf_op jit(solution)/shard_map/ppermute | solution.py:433
  16.2 3.6 %collective-permute-start.9 = (bf16[528,128]{1,0:T(8,128)(2,1)S(1)}, bf16[528,128]{1,0:T(8,128)(2,1)S(1)}, u32[]{:S(2)}, u32[]{:S(2)}) collective-permute-start(bf16[528,128]{1,0:T(8,128)(2,1)S(1)} %get-tuple-element.29), channel_id=1, source_target_pairs={{0,7},{1,6},{2,5},{3,4},{4,3},{5,2},{6,1},{7,0},{8,15},{9,14},{10,... | collective-permute-start | bytes 405512 | tf_op jit(solution)/shard_map/ppermute | solution.py:435
  19.8 3.3 %smooth.1 = (bf16[8,2,64,128]{3,2,1,0:T(8,128)(2,1)S(1)}, bf16[8,2,64,128]{3,2,1,0:T(8,128)(2,1)S(1)}, bf16[8,2,64,128]{3,2,1,0:T(8,128)(2,1)S(1)}, bf16[8,2,64,128]{3,2,1,0:T(8,128)(2,1)S(1)}) custom-call(s32[2,8]{1,0:T(2,128)S(1)} %bitcast.6, s32[4]{0:T(128)S(1)} %pad_add_fusion.place_ref, bf16[8,2,64,512]{3,2,1,0:T(8,128)(2,1)S(1)} %copy-done, ...), custom_call_target="tpu_custom_call" | custom-call | tf_op jit(solution)/shard_map/smooth/pallas_call | solution.py:208
  23.1 0.8 %collective-permute-start.2 = (bf16[8,2,64,128]{3,2,1,0:T(8,128)(2,1)S(1)}, bf16[8,2,64,128]{3,2,1,0:T(8,128)(2,1)S(1)}, u32[]{:S(2)}, u32[]{:S(2)}) collective-permute-start(bf16[8,2,64,128]{3,2,1,0:T(8,128)(2,1)S(1)} %get-tuple-element.21), channel_id=1, source_target_pairs={{0,24},{8,16},{16,8},{24,0},{1,25},{9,17},{17,9},{25,1},{2,26},{10... | collective-permute-start | bytes 786440 | tf_op jit(solution)/shard_map/ppermute | solution.py:440
  24.0 0.8 %collective-permute-start.3 = (bf16[8,2,64,128]{3,2,1,0:T(8,128)(2,1)S(1)}, bf16[8,2,64,128]{3,2,1,0:T(8,128)(2,1)S(1)}, u32[]{:S(2)}, u32[]{:S(2)}) collective-permute-start(bf16[8,2,64,128]{3,2,1,0:T(8,128)(2,1)S(1)} %get-tuple-element.22), channel_id=1, source_target_pairs={{0,16},{8,24},{16,0},{24,8},{1,17},{9,25},{17,1},{25,9},{2,18},{10... | collective-permute-start | bytes 786440 | tf_op jit(solution)/shard_map/ppermute | solution.py:440
  24.8 4.5 %collective-permute-done.7.refs_6_.refs_2_ = bf16[528,128]{1,0:T(8,128)(2,1)S(1)} collective-permute-done((bf16[528,128]{1,0:T(8,128)(2,1)S(1)}, bf16[528,128]{1,0:T(8,128)(2,1)S(1)}, u32[]{:S(2)}, u32[]{:S(2)}) %collective-permute-start.7) | collective-permute-done | bytes 135200 | tf_op jit(solution)/shard_map/ppermute | solution.py:435
  29.6 1.2 %collective-permute-start.10 = (bf16[528,128]{1,0:T(8,128)(2,1)S(1)}, bf16[528,128]{1,0:T(8,128)(2,1)S(1)}, u32[]{:S(2)}, u32[]{:S(2)}) collective-permute-start(bf16[528,128]{1,0:T(8,128)(2,1)S(1)} %get-tuple-element.30), channel_id=1, source_target_pairs={{0,5},{1,4},{2,7},{3,6},{4,1},{5,0},{6,3},{7,2},{8,13},{9,12},{10,... | collective-permute-start | bytes 405512 | tf_op jit(solution)/shard_map/ppermute | solution.py:435
  30.8 2.2 %collective-permute-start.11 = (bf16[528,128]{1,0:T(8,128)(2,1)S(1)}, bf16[528,128]{1,0:T(8,128)(2,1)S(1)}, u32[]{:S(2)}, u32[]{:S(2)}) collective-permute-start(bf16[528,128]{1,0:T(8,128)(2,1)S(1)} %get-tuple-element.31), channel_id=1, source_target_pairs={{0,3},{1,2},{2,1},{3,0},{4,7},{5,6},{6,5},{7,4},{8,11},{9,10},{10,... | collective-permute-start | bytes 405512 | tf_op jit(solution)/shard_map/ppermute | solution.py:435
  33.4 1.2 %spread_filters.1.spread_ref = bf16[2,512,512]{2,1,0:T(8,128)(2,1)S(1)} custom-call(s32[4]{0:T(128)S(1)} %pad_add_fusion.place_ref, bf16[2,32,32]{2,1,0:T(8,128)(2,1)S(1)} %multiply_reduce_fusion.kernel_ref), custom_call_target="tpu_custom_call" | custom-call | tf_op jit(solution)/shard_map/spread_filters/pallas_call | solution.py:246
  34.6 2.8 %collective-permute-done.3.refs_1_ = bf16[8,2,64,128]{3,2,1,0:T(8,128)(2,1)S(1)} collective-permute-done((bf16[8,2,64,128]{3,2,1,0:T(8,128)(2,1)S(1)}, bf16[8,2,64,128]{3,2,1,0:T(8,128)(2,1)S(1)}, u32[]{:S(2)}, u32[]{:S(2)}) %collective-permute-start.3) | collective-permute-done | bytes 262176 | tf_op jit(solution)/shard_map/ppermute | solution.py:440
  37.4 1.2 %deconvolve.1.spikes_ref = bf16[1,16,256,128]{3,2,1,0:T(8,128)(2,1)S(1)} custom-call(bf16[2,512,512]{2,1,0:T(8,128)(2,1)S(1)} %spread_filters.1.spread_ref, bf16[8,2,64,128]{3,2,1,0:T(8,128)(2,1)S(1)} %collective-permute-done.2.refs_0_, bf16[8,2,64,128]{3,2,1,0:T(8,128)(2,1)S(1)} %collective-permute-done.3.refs_1_, ...), custom_call_target="tpu_custom_call" | custom-call | tf_op jit(solution)/shard_map/deconvolve/pallas_call | solution.py:313
  38.6 1.3 %collective-permute-done.10.refs_5_ = bf16[528,128]{1,0:T(8,128)(2,1)S(1)} collective-permute-done((bf16[528,128]{1,0:T(8,128)(2,1)S(1)}, bf16[528,128]{1,0:T(8,128)(2,1)S(1)}, u32[]{:S(2)}, u32[]{:S(2)}) %collective-permute-start.10) | collective-permute-done | bytes 135200 | tf_op jit(solution)/shard_map/ppermute | solution.py:435
  40.3 1.4 %pool.1 = f32[32,8,128]{2,1,0:T(8,128)S(1)} custom-call(s32[4]{0:T(128)S(1)} %pad_add_fusion.place_ref, bf16[1,16,256,128]{3,2,1,0:T(8,128)(2,1)S(1)} %deconvolve.1.spikes_ref, bf16[528,128]{1,0:T(8,128)(2,1)S(1)} %collective-permute-done.5.refs_4_.refs_0_, bf16[528,128]{1,0:T(8,128)(2,1)S(1)} %collective-permute-done.6.refs_5_.refs_1_, ...), custom_call_target="tpu_custom_call" | custom-call | tf_op jit(solution)/shard_map/pool/pallas_call | solution.py:388
  41.8 11.1 %all_to_all.5.parts_ref = f32[32,8,128]{2,1,0:T(8,128)S(1)} all-to-all(f32[32,8,128]{2,1,0:T(8,128)S(1)} %pool.1), channel_id=1, replica_groups=mesh['frame'=4,'tile'=8] {'frame','tile'}, dimensions={0} | all-to-all | bytes 262144 | tf_op jit(solution)/shard_map/all_to_all | solution.py:444
  52.9 0.7 %finish.1 = f32[32,32]{1,0:T(8,128)} custom-call(f32[32,8,128]{2,1,0:T(8,128)S(1)} %all_to_all.5.parts_ref), custom_call_target="tpu_custom_call" | custom-call | tf_op jit(solution)/shard_map/finish/pallas_call | solution.py:407
  (24 shorter events, 1.1 us)
Async XLA Ops:
  0.1 1.2 %copy-start = (bf16[8,2,64,512]{3,2,1,0:T(8,128)(2,1)S(1)}, bf16[8,2,64,512]{3,2,1,0:T(8,128)(2,1)}, u32[]{:S(2)}) copy-start(bf16[8,2,64,512]{3,2,1,0:T(8,128)(2,1)} %movie_ref.3) | copy-start | bytes 3145732
  1.3 7.1 %copy-start.1 = (bf16[32,16384]{1,0:T(8,128)(2,1)S(1)}, bf16[32,16384]{1,0:T(8,128)(2,1)}, u32[]{:S(2)}) copy-start(bf16[32,16384]{1,0:T(8,128)(2,1)} %weights_ref.1) | copy-start | bytes 3145732
  2.0 12.1 %collective-permute-start = (bf16[8,24,512]{2,1,0:T(8,128)(2,1)S(1)}, bf16[8,24,512]{2,1,0:T(8,128)(2,1)S(1)}, u32[]{:S(2)}, u32[]{:S(2)}) collective-permute-start(bf16[8,24,512]{2,1,0:T(8,128)(2,1)S(1)} %get-tuple-element.19), channel_id=1, source_target_pairs={{1,2},{3,4},{5,6},{2,1},{4,3},{6,5},{9,10},{11,12},{13,14},{10,9},... | collective-permute-start | bytes 589832 | tf_op jit(solution)/shard_map/ppermute | solution.py:432
  2.7 13.5 %collective-permute-start.1 = (bf16[8,24,512]{2,1,0:T(8,128)(2,1)S(1)}, bf16[8,24,512]{2,1,0:T(8,128)(2,1)S(1)}, u32[]{:S(2)}, u32[]{:S(2)}) collective-permute-start(bf16[8,24,512]{2,1,0:T(8,128)(2,1)S(1)} %get-tuple-element.20), channel_id=1, source_target_pairs={{0,1},{1,0},{2,3},{3,2},{4,5},{5,4},{6,7},{7,6},{8,9},{9,8},{10,11... | collective-permute-start | bytes 589832 | tf_op jit(solution)/shard_map/ppermute | solution.py:433
  8.4 0.7 %copy-start.3 = (s32[32,1]{0,1:T(1,128)S(1)}, s32[32,1]{0,1:T(1,128)}, u32[]{:S(2)}) copy-start(s32[32,1]{0,1:T(1,128)} %param.10) | copy-start | bytes 388
  8.4 0.7 %copy-start.4 = (s32[32,1]{0,1:T(1,128)S(1)}, s32[32,1]{0,1:T(1,128)}, u32[]{:S(2)}) copy-start(s32[32,1]{0,1:T(1,128)} %param.11) | copy-start | bytes 388
  9.9 13.2 %collective-permute-start.5 = (bf16[528,128]{1,0:T(8,128)(2,1)S(1)}, bf16[528,128]{1,0:T(8,128)(2,1)S(1)}, u32[]{:S(2)}, u32[]{:S(2)}) collective-permute-start(bf16[528,128]{1,0:T(8,128)(2,1)S(1)} %get-tuple-element.25), channel_id=1, source_target_pairs={{0,2},{1,3},{2,0},{3,1},{4,6},{5,7},{6,4},{7,5},{8,10},{9,11},{10,... | collective-permute-start | bytes 405512 | tf_op jit(solution)/shard_map/ppermute | solution.py:435
  11.6 12.4 %collective-permute-start.6 = (bf16[528,128]{1,0:T(8,128)(2,1)S(1)}, bf16[528,128]{1,0:T(8,128)(2,1)S(1)}, u32[]{:S(2)}, u32[]{:S(2)}) collective-permute-start(bf16[528,128]{1,0:T(8,128)(2,1)S(1)} %get-tuple-element.26), channel_id=1, source_target_pairs={{0,6},{1,7},{2,4},{3,5},{4,2},{5,3},{6,0},{7,1},{8,14},{9,15},{10,... | collective-permute-start | bytes 405512 | tf_op jit(solution)/shard_map/ppermute | solution.py:435
  14.1 15.3 %collective-permute-start.7 = (bf16[528,128]{1,0:T(8,128)(2,1)S(1)}, bf16[528,128]{1,0:T(8,128)(2,1)S(1)}, u32[]{:S(2)}, u32[]{:S(2)}) collective-permute-start(bf16[528,128]{1,0:T(8,128)(2,1)S(1)} %get-tuple-element.27), channel_id=1, source_target_pairs={{0,4},{1,5},{2,6},{3,7},{4,0},{5,1},{6,2},{7,3},{8,12},{9,13},{10,... | collective-permute-start | bytes 405512 | tf_op jit(solution)/shard_map/ppermute | solution.py:435
  14.1 15.5 %collective-permute-start.8 = (bf16[528,128]{1,0:T(8,128)(2,1)S(1)}, bf16[528,128]{1,0:T(8,128)(2,1)S(1)}, u32[]{:S(2)}, u32[]{:S(2)}) collective-permute-start(bf16[528,128]{1,0:T(8,128)(2,1)S(1)} %get-tuple-element.28), channel_id=1, source_target_pairs={{0,1},{1,0},{2,3},{3,2},{4,5},{5,4},{6,7},{7,6},{8,9},{9,8},{10,11... | collective-permute-start | bytes 405512 | tf_op jit(solution)/shard_map/ppermute | solution.py:435
  16.2 3.6 %copy-start.2 = (s32[8,2]{0,1:T(2,128)S(1)}, s32[8,2]{0,1:T(2,128)}, u32[]{:S(2)}) copy-start(s32[8,2]{0,1:T(2,128)} %param.7) | copy-start | bytes 196
  16.2 14.6 %collective-permute-start.9 = (bf16[528,128]{1,0:T(8,128)(2,1)S(1)}, bf16[528,128]{1,0:T(8,128)(2,1)S(1)}, u32[]{:S(2)}, u32[]{:S(2)}) collective-permute-start(bf16[528,128]{1,0:T(8,128)(2,1)S(1)} %get-tuple-element.29), channel_id=1, source_target_pairs={{0,7},{1,6},{2,5},{3,4},{4,3},{5,2},{6,1},{7,0},{8,15},{9,14},{10,... | collective-permute-start | bytes 405512 | tf_op jit(solution)/shard_map/ppermute | solution.py:435
  23.1 11.5 %collective-permute-start.2 = (bf16[8,2,64,128]{3,2,1,0:T(8,128)(2,1)S(1)}, bf16[8,2,64,128]{3,2,1,0:T(8,128)(2,1)S(1)}, u32[]{:S(2)}, u32[]{:S(2)}) collective-permute-start(bf16[8,2,64,128]{3,2,1,0:T(8,128)(2,1)S(1)} %get-tuple-element.21), channel_id=1, source_target_pairs={{0,24},{8,16},{16,8},{24,0},{1,25},{9,17},{17,9},{25,1},{2,26},{10... | collective-permute-start | bytes 786440 | tf_op jit(solution)/shard_map/ppermute | solution.py:440
  24.0 13.5 %collective-permute-start.3 = (bf16[8,2,64,128]{3,2,1,0:T(8,128)(2,1)S(1)}, bf16[8,2,64,128]{3,2,1,0:T(8,128)(2,1)S(1)}, u32[]{:S(2)}, u32[]{:S(2)}) collective-permute-start(bf16[8,2,64,128]{3,2,1,0:T(8,128)(2,1)S(1)} %get-tuple-element.22), channel_id=1, source_target_pairs={{0,16},{8,24},{16,0},{24,8},{1,17},{9,25},{17,1},{25,9},{2,18},{10... | collective-permute-start | bytes 786440 | tf_op jit(solution)/shard_map/ppermute | solution.py:440
  29.3 8.1 %collective-permute-start.4 = (bf16[8,2,64,128]{3,2,1,0:T(8,128)(2,1)S(1)}, bf16[8,2,64,128]{3,2,1,0:T(8,128)(2,1)S(1)}, u32[]{:S(2)}, u32[]{:S(2)}) collective-permute-start(bf16[8,2,64,128]{3,2,1,0:T(8,128)(2,1)S(1)} %get-tuple-element.23), channel_id=1, source_target_pairs={{0,8},{8,0},{16,24},{24,16},{1,9},{9,1},{17,25},{25,17},{2,10},{10... | collective-permute-start | bytes 786440 | tf_op jit(solution)/shard_map/ppermute | solution.py:440
  29.6 3.5 %copy-start.5 = (f32[2,64]{1,0:T(2,128)S(1)}, f32[2,64]{1,0:T(2,128)}, u32[]{:S(2)}) copy-start(f32[2,64]{1,0:T(2,128)} %param.8) | copy-start | bytes 1540
  29.6 10.4 %collective-permute-start.10 = (bf16[528,128]{1,0:T(8,128)(2,1)S(1)}, bf16[528,128]{1,0:T(8,128)(2,1)S(1)}, u32[]{:S(2)}, u32[]{:S(2)}) collective-permute-start(bf16[528,128]{1,0:T(8,128)(2,1)S(1)} %get-tuple-element.30), channel_id=1, source_target_pairs={{0,5},{1,4},{2,7},{3,6},{4,1},{5,0},{6,3},{7,2},{8,13},{9,12},{10,... | collective-permute-start | bytes 405512 | tf_op jit(solution)/shard_map/ppermute | solution.py:435
  30.8 9.5 %collective-permute-start.11 = (bf16[528,128]{1,0:T(8,128)(2,1)S(1)}, bf16[528,128]{1,0:T(8,128)(2,1)S(1)}, u32[]{:S(2)}, u32[]{:S(2)}) collective-permute-start(bf16[528,128]{1,0:T(8,128)(2,1)S(1)} %get-tuple-element.31), channel_id=1, source_target_pairs={{0,3},{1,2},{2,1},{3,0},{4,7},{5,6},{6,5},{7,4},{8,11},{9,10},{10,... | collective-permute-start | bytes 405512 | tf_op jit(solution)/shard_map/ppermute | solution.py:435

commit v3 on v2

--- a/solution.py
+++ b/solution.py
@@ -424,7 +424,7 @@
     tile = lax.axis_index("tile")
     place = jnp.stack([tile * rows, tiles * rows, lax.axis_index("frame"), tile]).astype(jnp.int32)
     far, close = list(range(tiles // 2, tiles)), list(range(1, tiles // 2))
-    order = close[1:2] + far[-2:-1] + far[:1] + close[:1] + far[-1:] + far[-3:0:-1] + close[2:] + [0]
+    order = far[-2:-1] + close[1:2] + far[:1] + close[:1] + far[-1:] + far[-3:0:-1] + close[2:] + [0]
     owner, local = slot_owner.reshape(1, slots), slot_local.reshape(1, slots)
     pair, other = edges(movie, place)
     packed = pack(weights, owner, local, order, planes, place)

time: 53.8 us -> 54 us (level)
  blocking collectives: 11.1 us -> 12 us
  waiting for transfers between devices: 9.79 us -> 9.23 us
    ppermute x7, waiting for transfers between devices: 6.23 us -> 3.7 us  [body(): lax.ppermute(cells, 'tile', [(i, i ^ k) for i in range(tiles)])]
    ppermute x3, waiting for transfers between devices: 2.77 us -> 3.97 us  [body(): lax.ppermute(pieces[k], 'frame', [(i, i ^ k) for i in range(parts)])]
    all_to_all x1, blocking collectives: 11.1 us -> 12 us  [body(): lax.all_to_all(traces, ('frame', 'tile'), split_axis=0, concat_axis=0, ti...]
    ppermute x1, waiting for transfers between devices: 0.79 us -> 1.55 us  [body(): pair = lax.ppermute(pair, 'tile', [(i, i ^ 1) for i in range(tiles)])]
  transfers between devices with their start and end apart: 12 -> 12, of which waited for: 5 -> 3; matrix products, arithmetic and copies ran while one was open for 1% -> 1% of each run, Pallas kernels for 12% -> 12%
where the time goes in v3:
time: 54 us; the launch traced here: 53.8 us
  starting transfers between devices  20.4 us (38%)
  blocking collectives  12 us (22%)
  Pallas kernels  9.41 us (17%)
  waiting for transfers between devices  9.23 us (17%)
  local copies, waits for them, and re-layouts  1.91 us (4%)
  other arithmetic  0.64 us (1%)
    ppermute x7, starting transfers between devices, body(): lax.ppermute(cells, 'tile', [(i, i ^ k) for i in range(tiles)])  12.3 us
    all_to_all x1, blocking collectives, body(): lax.all_to_all(traces, ('frame', 'tile'), split_axis=0, concat_axis=0, ti...  12 us
    ppermute x1, starting transfers between devices, body(): pair = lax.ppermute(pair, 'tile', [(i, i ^ 1) for i in range(tiles)])  5.79 us
    ppermute x3, waiting for transfers between devices, body(): lax.ppermute(pieces[k], 'frame', [(i, i ^ k) for i in range(parts)])  3.97 us
    ppermute x7, waiting for transfers between devices, body(): lax.ppermute(cells, 'tile', [(i, i ^ k) for i in range(tiles)])  3.7 us
    pallas_call x1, Pallas kernels, smooth(): pl.pallas_call(smooth_kernel, out_shape=[jax.ShapeDtypeStruct((frames, pl...  3.35 us
    unnamed x12, local copies, waits for them, and re-layouts  1.91 us
    ppermute x3, starting transfers between devices, body(): lax.ppermute(pieces[k], 'frame', [(i, i ^ k) for i in range(parts)])  1.66 us
  transfers between devices with their start and end apart: 12, of which 3 were waited for; matrix products, arithmetic and copies ran while one was open for 1% of the time, Pallas kernels for 12%

profile of v3, /device:TPU:0, one launch (start us, length us, event | category | flops | bytes accessed | tf_op | source)
XLA Modules:
  0.0 53.8 jit_solution(14913824283970414618)
XLA Ops:
  0.1 1.2 %copy-done = bf16[8,2,64,512]{3,2,1,0:T(8,128)(2,1)S(1)} copy-done((bf16[8,2,64,512]{3,2,1,0:T(8,128)(2,1)S(1)}, bf16[8,2,64,512]{3,2,1,0:T(8,128)(2,1)}, u32[]{:S(2)}) %copy-start) | copy-done | bytes 1048600
  1.3 0.7 %edges.1 = (bf16[8,24,512]{2,1,0:T(8,128)(2,1)S(1)}, bf16[8,24,512]{2,1,0:T(8,128)(2,1)S(1)}) custom-call(s32[4]{0:T(128)S(1)} %pad_add_fusion.place_ref, bf16[8,2,64,512]{3,2,1,0:T(8,128)(2,1)S(1)} %copy-done), custom_call_target="tpu_custom_call" | custom-call | tf_op jit(solution)/shard_map/edges/pallas_call | solution.py:69
  2.0 0.7 %collective-permute-start = (bf16[8,24,512]{2,1,0:T(8,128)(2,1)S(1)}, bf16[8,24,512]{2,1,0:T(8,128)(2,1)S(1)}, u32[]{:S(2)}, u32[]{:S(2)}) collective-permute-start(bf16[8,24,512]{2,1,0:T(8,128)(2,1)S(1)} %get-tuple-element.19), channel_id=1, source_target_pairs={{1,2},{3,4},{5,6},{2,1},{4,3},{6,5},{9,10},{11,12},{13,14},{10,9},... | collective-permute-start | bytes 589832 | tf_op jit(solution)/shard_map/ppermute | solution.py:432
  2.7 5.8 %collective-permute-start.1 = (bf16[8,24,512]{2,1,0:T(8,128)(2,1)S(1)}, bf16[8,24,512]{2,1,0:T(8,128)(2,1)S(1)}, u32[]{:S(2)}, u32[]{:S(2)}) collective-permute-start(bf16[8,24,512]{2,1,0:T(8,128)(2,1)S(1)} %get-tuple-element.20), channel_id=1, source_target_pairs={{0,1},{1,0},{2,3},{3,2},{4,5},{5,4},{6,7},{7,6},{8,9},{9,8},{10,11... | collective-permute-start | bytes 589832 | tf_op jit(solution)/shard_map/ppermute | solution.py:433
  8.5 0.6 %copy-done.3 = s32[32,1]{0,1:T(1,128)S(1)} copy-done((s32[32,1]{0,1:T(1,128)S(1)}, s32[32,1]{0,1:T(1,128)}, u32[]{:S(2)}) %copy-start.3) | copy-done | bytes 152
  9.1 0.8 %pack_weights.1 = (bf16[528,128]{1,0:T(8,128)(2,1)S(1)}, bf16[528,128]{1,0:T(8,128)(2,1)S(1)}, bf16[528,128]{1,0:T(8,128)(2,1)S(1)}, bf16[528,128]{1,0:T(8,128)(...) custom-call(s32[4]{0:T(128)S(1)} %pad_add_fusion.place_ref, ...), custom_call_target="tpu_custom_call" | custom-call | tf_op jit(solution)/shard_map/pack_weights/pallas_call | solution.py:102
  9.9 2.0 %collective-permute-start.5 = (bf16[528,128]{1,0:T(8,128)(2,1)S(1)}, bf16[528,128]{1,0:T(8,128)(2,1)S(1)}, u32[]{:S(2)}, u32[]{:S(2)}) collective-permute-start(bf16[528,128]{1,0:T(8,128)(2,1)S(1)} %get-tuple-element.25), channel_id=1, source_target_pairs={{0,6},{1,7},{2,4},{3,5},{4,2},{5,3},{6,0},{7,1},{8,14},{9,15},{10,... | collective-permute-start | bytes 405512 | tf_op jit(solution)/shard_map/ppermute | solution.py:435
  12.0 1.2 %collective-permute-start.6 = (bf16[528,128]{1,0:T(8,128)(2,1)S(1)}, bf16[528,128]{1,0:T(8,128)(2,1)S(1)}, u32[]{:S(2)}, u32[]{:S(2)}) collective-permute-start(bf16[528,128]{1,0:T(8,128)(2,1)S(1)} %get-tuple-element.26), channel_id=1, source_target_pairs={{0,2},{1,3},{2,0},{3,1},{4,6},{5,7},{6,4},{7,5},{8,10},{9,11},{10,... | collective-permute-start | bytes 405512 | tf_op jit(solution)/shard_map/ppermute | solution.py:435
  13.2 1.2 %collective-permute-start.7 = (bf16[528,128]{1,0:T(8,128)(2,1)S(1)}, bf16[528,128]{1,0:T(8,128)(2,1)S(1)}, u32[]{:S(2)}, u32[]{:S(2)}) collective-permute-start(bf16[528,128]{1,0:T(8,128)(2,1)S(1)} %get-tuple-element.27), channel_id=1, source_target_pairs={{0,4},{1,5},{2,6},{3,7},{4,0},{5,1},{6,2},{7,3},{8,12},{9,13},{10,... | collective-permute-start | bytes 405512 | tf_op jit(solution)/shard_map/ppermute | solution.py:435
  14.4 0.2 collective-permute-start.8
  14.6 1.5 %collective-permute-done.1.pair_ref = bf16[8,24,512]{2,1,0:T(8,128)(2,1)S(1)} collective-permute-done((bf16[8,24,512]{2,1,0:T(8,128)(2,1)S(1)}, bf16[8,24,512]{2,1,0:T(8,128)(2,1)S(1)}, u32[]{:S(2)}, u32[]{:S(2)}) %collective-permute-start.1) | collective-permute-done | bytes 196640 | tf_op jit(solution)/shard_map/ppermute | solution.py:433
  16.2 4.5 %collective-permute-start.9 = (bf16[528,128]{1,0:T(8,128)(2,1)S(1)}, bf16[528,128]{1,0:T(8,128)(2,1)S(1)}, u32[]{:S(2)}, u32[]{:S(2)}) collective-permute-start(bf16[528,128]{1,0:T(8,128)(2,1)S(1)} %get-tuple-element.29), channel_id=1, source_target_pairs={{0,7},{1,6},{2,5},{3,4},{4,3},{5,2},{6,1},{7,0},{8,15},{9,14},{10,... | collective-permute-start | bytes 405512 | tf_op jit(solution)/shard_map/ppermute | solution.py:435
  20.7 3.3 %smooth.1 = (bf16[8,2,64,128]{3,2,1,0:T(8,128)(2,1)S(1)}, bf16[8,2,64,128]{3,2,1,0:T(8,128)(2,1)S(1)}, bf16[8,2,64,128]{3,2,1,0:T(8,128)(2,1)S(1)}, bf16[8,2,64,128]{3,2,1,0:T(8,128)(2,1)S(1)}) custom-call(s32[2,8]{1,0:T(2,128)S(1)} %bitcast.6, s32[4]{0:T(128)S(1)} %pad_add_fusion.place_ref, bf16[8,2,64,512]{3,2,1,0:T(8,128)(2,1)S(1)} %copy-done, ...), custom_call_target="tpu_custom_call" | custom-call | tf_op jit(solution)/shard_map/smooth/pallas_call | solution.py:208
  24.1 1.6 %collective-permute-start.3 = (bf16[8,2,64,128]{3,2,1,0:T(8,128)(2,1)S(1)}, bf16[8,2,64,128]{3,2,1,0:T(8,128)(2,1)S(1)}, u32[]{:S(2)}, u32[]{:S(2)}) collective-permute-start(bf16[8,2,64,128]{3,2,1,0:T(8,128)(2,1)S(1)} %get-tuple-element.22), channel_id=1, source_target_pairs={{0,16},{8,24},{16,0},{24,8},{1,17},{9,25},{17,1},{25,9},{2,18},{10... | collective-permute-start | bytes 786440 | tf_op jit(solution)/shard_map/ppermute | solution.py:440
  25.7 3.7 %collective-permute-done.7.refs_6_.refs_2_ = bf16[528,128]{1,0:T(8,128)(2,1)S(1)} collective-permute-done((bf16[528,128]{1,0:T(8,128)(2,1)S(1)}, bf16[528,128]{1,0:T(8,128)(2,1)S(1)}, u32[]{:S(2)}, u32[]{:S(2)}) %collective-permute-start.7) | collective-permute-done | bytes 135200 | tf_op jit(solution)/shard_map/ppermute | solution.py:435
  29.6 0.7 %collective-permute-start.10 = (bf16[528,128]{1,0:T(8,128)(2,1)S(1)}, bf16[528,128]{1,0:T(8,128)(2,1)S(1)}, u32[]{:S(2)}, u32[]{:S(2)}) collective-permute-start(bf16[528,128]{1,0:T(8,128)(2,1)S(1)} %get-tuple-element.30), channel_id=1, source_target_pairs={{0,5},{1,4},{2,7},{3,6},{4,1},{5,0},{6,3},{7,2},{8,13},{9,12},{10,... | collective-permute-start | bytes 405512 | tf_op jit(solution)/shard_map/ppermute | solution.py:435
  30.4 2.4 %collective-permute-start.11 = (bf16[528,128]{1,0:T(8,128)(2,1)S(1)}, bf16[528,128]{1,0:T(8,128)(2,1)S(1)}, u32[]{:S(2)}, u32[]{:S(2)}) collective-permute-start(bf16[528,128]{1,0:T(8,128)(2,1)S(1)} %get-tuple-element.31), channel_id=1, source_target_pairs={{0,3},{1,2},{2,1},{3,0},{4,7},{5,6},{6,5},{7,4},{8,11},{9,10},{10,... | collective-permute-start | bytes 405512 | tf_op jit(solution)/shard_map/ppermute | solution.py:435
  32.8 0.4 multiply_reduce_fusion.kernel_ref
  33.1 1.2 %spread_filters.1.spread_ref = bf16[2,512,512]{2,1,0:T(8,128)(2,1)S(1)} custom-call(s32[4]{0:T(128)S(1)} %pad_add_fusion.place_ref, bf16[2,32,32]{2,1,0:T(8,128)(2,1)S(1)} %multiply_reduce_fusion.kernel_ref), custom_call_target="tpu_custom_call" | custom-call | tf_op jit(solution)/shard_map/spread_filters/pallas_call | solution.py:246
  34.4 4.0 %collective-permute-done.3.refs_1_ = bf16[8,2,64,128]{3,2,1,0:T(8,128)(2,1)S(1)} collective-permute-done((bf16[8,2,64,128]{3,2,1,0:T(8,128)(2,1)S(1)}, bf16[8,2,64,128]{3,2,1,0:T(8,128)(2,1)S(1)}, u32[]{:S(2)}, u32[]{:S(2)}) %collective-permute-start.3) | collective-permute-done | bytes 262176 | tf_op jit(solution)/shard_map/ppermute | solution.py:440
  38.3 1.2 %deconvolve.1.spikes_ref = bf16[1,16,256,128]{3,2,1,0:T(8,128)(2,1)S(1)} custom-call(bf16[2,512,512]{2,1,0:T(8,128)(2,1)S(1)} %spread_filters.1.spread_ref, bf16[8,2,64,128]{3,2,1,0:T(8,128)(2,1)S(1)} %collective-permute-done.2.refs_0_, bf16[8,2,64,128]{3,2,1,0:T(8,128)(2,1)S(1)} %collective-permute-done.3.refs_1_, ...), custom_call_target="tpu_custom_call" | custom-call | tf_op jit(solution)/shard_map/deconvolve/pallas_call | solution.py:313
  39.6 1.4 %pool.1 = f32[32,8,128]{2,1,0:T(8,128)S(1)} custom-call(s32[4]{0:T(128)S(1)} %pad_add_fusion.place_ref, bf16[1,16,256,128]{3,2,1,0:T(8,128)(2,1)S(1)} %deconvolve.1.spikes_ref, bf16[528,128]{1,0:T(8,128)(2,1)S(1)} %collective-permute-done.5.refs_4_.refs_0_, bf16[528,128]{1,0:T(8,128)(2,1)S(1)} %collective-permute-done.6.refs_5_.refs_1_, ...), custom_call_target="tpu_custom_call" | custom-call | tf_op jit(solution)/shard_map/pool/pallas_call | solution.py:388
  41.0 12.0 %all_to_all.5.parts_ref = f32[32,8,128]{2,1,0:T(8,128)S(1)} all-to-all(f32[32,8,128]{2,1,0:T(8,128)S(1)} %pool.1), channel_id=1, replica_groups=mesh['frame'=4,'tile'=8] {'frame','tile'}, dimensions={0} | all-to-all | bytes 262144 | tf_op jit(solution)/shard_map/all_to_all | solution.py:444
  53.1 0.7 %finish.1 = f32[32,32]{1,0:T(8,128)} custom-call(f32[32,8,128]{2,1,0:T(8,128)S(1)} %all_to_all.5.parts_ref), custom_call_target="tpu_custom_call" | custom-call | tf_op jit(solution)/shard_map/finish/pallas_call | solution.py:407
  (24 shorter events, 0.4 us)
Async XLA Ops:
  0.1 1.2 %copy-start = (bf16[8,2,64,512]{3,2,1,0:T(8,128)(2,1)S(1)}, bf16[8,2,64,512]{3,2,1,0:T(8,128)(2,1)}, u32[]{:S(2)}) copy-start(bf16[8,2,64,512]{3,2,1,0:T(8,128)(2,1)} %movie_ref.3) | copy-start | bytes 3145732
  1.3 7.1 %copy-start.1 = (bf16[32,16384]{1,0:T(8,128)(2,1)S(1)}, bf16[32,16384]{1,0:T(8,128)(2,1)}, u32[]{:S(2)}) copy-start(bf16[32,16384]{1,0:T(8,128)(2,1)} %weights_ref.1) | copy-start | bytes 3145732
  2.0 12.4 %collective-permute-start = (bf16[8,24,512]{2,1,0:T(8,128)(2,1)S(1)}, bf16[8,24,512]{2,1,0:T(8,128)(2,1)S(1)}, u32[]{:S(2)}, u32[]{:S(2)}) collective-permute-start(bf16[8,24,512]{2,1,0:T(8,128)(2,1)S(1)} %get-tuple-element.19), channel_id=1, source_target_pairs={{1,2},{3,4},{5,6},{2,1},{4,3},{6,5},{9,10},{11,12},{13,14},{10,9},... | collective-permute-start | bytes 589832 | tf_op jit(solution)/shard_map/ppermute | solution.py:432
  2.7 13.5 %collective-permute-start.1 = (bf16[8,24,512]{2,1,0:T(8,128)(2,1)S(1)}, bf16[8,24,512]{2,1,0:T(8,128)(2,1)S(1)}, u32[]{:S(2)}, u32[]{:S(2)}) collective-permute-start(bf16[8,24,512]{2,1,0:T(8,128)(2,1)S(1)} %get-tuple-element.20), channel_id=1, source_target_pairs={{0,1},{1,0},{2,3},{3,2},{4,5},{5,4},{6,7},{7,6},{8,9},{9,8},{10,11... | collective-permute-start | bytes 589832 | tf_op jit(solution)/shard_map/ppermute | solution.py:433
  8.4 0.7 %copy-start.3 = (s32[32,1]{0,1:T(1,128)S(1)}, s32[32,1]{0,1:T(1,128)}, u32[]{:S(2)}) copy-start(s32[32,1]{0,1:T(1,128)} %param.10) | copy-start | bytes 388
  8.4 0.7 %copy-start.4 = (s32[32,1]{0,1:T(1,128)S(1)}, s32[32,1]{0,1:T(1,128)}, u32[]{:S(2)}) copy-start(s32[32,1]{0,1:T(1,128)} %param.11) | copy-start | bytes 388
  9.9 14.1 %collective-permute-start.5 = (bf16[528,128]{1,0:T(8,128)(2,1)S(1)}, bf16[528,128]{1,0:T(8,128)(2,1)S(1)}, u32[]{:S(2)}, u32[]{:S(2)}) collective-permute-start(bf16[528,128]{1,0:T(8,128)(2,1)S(1)} %get-tuple-element.25), channel_id=1, source_target_pairs={{0,6},{1,7},{2,4},{3,5},{4,2},{5,3},{6,0},{7,1},{8,14},{9,15},{10,... | collective-permute-start | bytes 405512 | tf_op jit(solution)/shard_map/ppermute | solution.py:435
  12.0 12.2 %collective-permute-start.6 = (bf16[528,128]{1,0:T(8,128)(2,1)S(1)}, bf16[528,128]{1,0:T(8,128)(2,1)S(1)}, u32[]{:S(2)}, u32[]{:S(2)}) collective-permute-start(bf16[528,128]{1,0:T(8,128)(2,1)S(1)} %get-tuple-element.26), channel_id=1, source_target_pairs={{0,2},{1,3},{2,0},{3,1},{4,6},{5,7},{6,4},{7,5},{8,10},{9,11},{10,... | collective-permute-start | bytes 405512 | tf_op jit(solution)/shard_map/ppermute | solution.py:435
  13.2 16.3 %collective-permute-start.7 = (bf16[528,128]{1,0:T(8,128)(2,1)S(1)}, bf16[528,128]{1,0:T(8,128)(2,1)S(1)}, u32[]{:S(2)}, u32[]{:S(2)}) collective-permute-start(bf16[528,128]{1,0:T(8,128)(2,1)S(1)} %get-tuple-element.27), channel_id=1, source_target_pairs={{0,4},{1,5},{2,6},{3,7},{4,0},{5,1},{6,2},{7,3},{8,12},{9,13},{10,... | collective-permute-start | bytes 405512 | tf_op jit(solution)/shard_map/ppermute | solution.py:435
  14.4 15.2 %collective-permute-start.8 = (bf16[528,128]{1,0:T(8,128)(2,1)S(1)}, bf16[528,128]{1,0:T(8,128)(2,1)S(1)}, u32[]{:S(2)}, u32[]{:S(2)}) collective-permute-start(bf16[528,128]{1,0:T(8,128)(2,1)S(1)} %get-tuple-element.28), channel_id=1, source_target_pairs={{0,1},{1,0},{2,3},{3,2},{4,5},{5,4},{6,7},{7,6},{8,9},{9,8},{10,11... | collective-permute-start | bytes 405512 | tf_op jit(solution)/shard_map/ppermute | solution.py:435
  16.2 4.5 %copy-start.2 = (s32[8,2]{0,1:T(2,128)S(1)}, s32[8,2]{0,1:T(2,128)}, u32[]{:S(2)}) copy-start(s32[8,2]{0,1:T(2,128)} %param.7) | copy-start | bytes 196
  16.2 14.2 %collective-permute-start.9 = (bf16[528,128]{1,0:T(8,128)(2,1)S(1)}, bf16[528,128]{1,0:T(8,128)(2,1)S(1)}, u32[]{:S(2)}, u32[]{:S(2)}) collective-permute-start(bf16[528,128]{1,0:T(8,128)(2,1)S(1)} %get-tuple-element.29), channel_id=1, source_target_pairs={{0,7},{1,6},{2,5},{3,4},{4,3},{5,2},{6,1},{7,0},{8,15},{9,14},{10,... | collective-permute-start | bytes 405512 | tf_op jit(solution)/shard_map/ppermute | solution.py:435
  24.1 10.3 %collective-permute-start.2 = (bf16[8,2,64,128]{3,2,1,0:T(8,128)(2,1)S(1)}, bf16[8,2,64,128]{3,2,1,0:T(8,128)(2,1)S(1)}, u32[]{:S(2)}, u32[]{:S(2)}) collective-permute-start(bf16[8,2,64,128]{3,2,1,0:T(8,128)(2,1)S(1)} %get-tuple-element.21), channel_id=1, source_target_pairs={{0,24},{8,16},{16,8},{24,0},{1,25},{9,17},{17,9},{25,1},{2,26},{10... | collective-permute-start | bytes 786440 | tf_op jit(solution)/shard_map/ppermute | solution.py:440
  24.1 14.2 %collective-permute-start.3 = (bf16[8,2,64,128]{3,2,1,0:T(8,128)(2,1)S(1)}, bf16[8,2,64,128]{3,2,1,0:T(8,128)(2,1)S(1)}, u32[]{:S(2)}, u32[]{:S(2)}) collective-permute-start(bf16[8,2,64,128]{3,2,1,0:T(8,128)(2,1)S(1)} %get-tuple-element.22), channel_id=1, source_target_pairs={{0,16},{8,24},{16,0},{24,8},{1,17},{9,25},{17,1},{25,9},{2,18},{10... | collective-permute-start | bytes 786440 | tf_op jit(solution)/shard_map/ppermute | solution.py:440
  29.4 8.9 %collective-permute-start.4 = (bf16[8,2,64,128]{3,2,1,0:T(8,128)(2,1)S(1)}, bf16[8,2,64,128]{3,2,1,0:T(8,128)(2,1)S(1)}, u32[]{:S(2)}, u32[]{:S(2)}) collective-permute-start(bf16[8,2,64,128]{3,2,1,0:T(8,128)(2,1)S(1)} %get-tuple-element.23), channel_id=1, source_target_pairs={{0,8},{8,0},{16,24},{24,16},{1,9},{9,1},{17,25},{25,17},{2,10},{10... | collective-permute-start | bytes 786440 | tf_op jit(solution)/shard_map/ppermute | solution.py:440
  29.6 3.2 %copy-start.5 = (f32[2,64]{1,0:T(2,128)S(1)}, f32[2,64]{1,0:T(2,128)}, u32[]{:S(2)}) copy-start(f32[2,64]{1,0:T(2,128)} %param.8) | copy-start | bytes 1540
  29.6 9.9 %collective-permute-start.10 = (bf16[528,128]{1,0:T(8,128)(2,1)S(1)}, bf16[528,128]{1,0:T(8,128)(2,1)S(1)}, u32[]{:S(2)}, u32[]{:S(2)}) collective-permute-start(bf16[528,128]{1,0:T(8,128)(2,1)S(1)} %get-tuple-element.30), channel_id=1, source_target_pairs={{0,5},{1,4},{2,7},{3,6},{4,1},{5,0},{6,3},{7,2},{8,13},{9,12},{10,... | collective-permute-start | bytes 405512 | tf_op jit(solution)/shard_map/ppermute | solution.py:435
  30.4 9.2 %collective-permute-start.11 = (bf16[528,128]{1,0:T(8,128)(2,1)S(1)}, bf16[528,128]{1,0:T(8,128)(2,1)S(1)}, u32[]{:S(2)}, u32[]{:S(2)}) collective-permute-start(bf16[528,128]{1,0:T(8,128)(2,1)S(1)} %get-tuple-element.31), channel_id=1, source_target_pairs={{0,3},{1,2},{2,1},{3,0},{4,7},{5,6},{6,5},{7,4},{8,11},{9,10},{10,... | collective-permute-start | bytes 405512 | tf_op jit(solution)/shard_map/ppermute | solution.py:435

commit v4 on v2

--- a/solution.py
+++ b/solution.py
@@ -76,9 +76,8 @@
     )(place, movie)
 
 
-def pack_kernel(order, planes, place_ref, weights_ref, owner_ref, local_ref, *refs):
-    *out_refs, ids = refs
-    tiles = len(order)
+def pack_kernel(order, tiles, planes, place_ref, weights_ref, owner_ref, local_ref, *refs):
+    *out_refs, ids = refs[-1 - len(order) :]
     slots, pixels = weights_ref.shape
     octets = pixels // (planes * tiles * LANES)
     tail = planes * octets * slots
@@ -95,19 +94,18 @@
         out_ref[tail:, :] = ids[...].astype(jnp.bfloat16)
 
 
-def pack(weights, owner, local, order, planes, place):
+def pack(weights, owner, local, order, tiles, planes, place, *after):
     slots, pixels = weights.shape
-    tiles = len(order)
     shape = jax.ShapeDtypeStruct((pixels // (tiles * LANES) * slots + GROUP, LANES), jnp.bfloat16)
     return pl.pallas_call(
-        functools.partial(pack_kernel, order, planes),
-        out_shape=[shape] * tiles,
-        in_specs=[pl.BlockSpec(memory_space=pltpu.SMEM)] + whole_vmem(3),
-        out_specs=whole_vmem(tiles),
+        functools.partial(pack_kernel, order, tiles, planes),
+        out_shape=[shape] * len(order),
+        in_specs=[pl.BlockSpec(memory_space=pltpu.SMEM)] + whole_vmem(3) + [pl.BlockSpec(memory_space=pl.ANY)] * len(after),
+        out_specs=whole_vmem(len(order)),
         scratch_shapes=[pltpu.VMEM((GROUP, LANES), jnp.float32)],
         compiler_params=params(8 * MIB + 5 * weights.size),
         name="pack_weights",
-    )(place, weights, owner, local)
+    )(place, weights, owner, local, *after)
 
 
 def smooth_kernel(shift_ref, place_ref, movie_ref, other_ref, pair_ref, *refs):
@@ -427,10 +425,11 @@
     order = close[1:2] + far[-2:-1] + far[:1] + close[:1] + far[-1:] + far[-3:0:-1] + close[2:] + [0]
     owner, local = slot_owner.reshape(1, slots), slot_local.reshape(1, slots)
     pair, other = edges(movie, place)
-    packed = pack(weights, owner, local, order, planes, place)
     swaps = [(i, i + 1) for i in range(1, ends, 2)]
     other = lax.ppermute(other, "tile", swaps + [(j, i) for i, j in swaps])
     pair = lax.ppermute(pair, "tile", [(i, i ^ 1) for i in range(tiles)])
+    packed = pack(weights, owner, local, order[:3], tiles, planes, place)
+    packed += pack(weights, owner, local, order[3:], tiles, planes, place, other)
     landed = [
         lax.ppermute(cells, "tile", [(i, i ^ k) for i in range(tiles)]) if k else cells
         for k, cells in zip(order, packed)

time: 53.8 us -> 53.8 us (level)
  waiting for transfers between devices: 9.79 us -> 8.76 us
  Pallas kernels: 9.41 us -> 9.97 us
    ppermute x1, waiting for transfers between devices: 0.79 us -> 0.01 us  [body(): pair = lax.ppermute(pair, 'tile', [(i, i ^ 1) for i in range(tiles)])]
    ppermute x7, waiting for transfers between devices: 6.23 us -> 5.67 us  [body(): lax.ppermute(cells, 'tile', [(i, i ^ k) for i in range(tiles)])]
    pallas_call x1 -> x2, Pallas kernels: 0.82 us -> 1.37 us  [pack(): pl.pallas_call(functools.partial(pack_kernel, order, tiles, planes), out_...]
  transfers between devices with their start and end apart: 12 -> 12, of which waited for: 5 -> 4; matrix products, arithmetic and copies ran while one was open for 1% -> 1% of each run, Pallas kernels for 12% -> 13%
where the time goes in v4:
time: 53.8 us; the launch traced here: 53.6 us
  starting transfers between devices  21 us (39%)
  blocking collectives  11.1 us (21%)
  Pallas kernels  9.97 us (19%)
  waiting for transfers between devices  8.76 us (16%)
  local copies, waits for them, and re-layouts  1.98 us (4%)
  other arithmetic  0.64 us (1%)
    ppermute x7, starting transfers between devices, body(): lax.ppermute(cells, 'tile', [(i, i ^ k) for i in range(tiles)])  12.9 us
    all_to_all x1, blocking collectives, body(): lax.all_to_all(traces, ('frame', 'tile'), split_axis=0, concat_axis=0, ti...  11.1 us
    ppermute x1, starting transfers between devices, body(): pair = lax.ppermute(pair, 'tile', [(i, i ^ 1) for i in range(tiles)])  5.79 us
    ppermute x7, waiting for transfers between devices, body(): lax.ppermute(cells, 'tile', [(i, i ^ k) for i in range(tiles)])  5.67 us
    pallas_call x1, Pallas kernels, smooth(): pl.pallas_call(smooth_kernel, out_shape=[jax.ShapeDtypeStruct((frames, pl...  3.34 us
    ppermute x3, waiting for transfers between devices, body(): lax.ppermute(pieces[k], 'frame', [(i, i ^ k) for i in range(parts)])  3.09 us
    unnamed x12, local copies, waits for them, and re-layouts  1.98 us
    ppermute x3, starting transfers between devices, body(): lax.ppermute(pieces[k], 'frame', [(i, i ^ k) for i in range(parts)])  1.68 us
  transfers between devices with their start and end apart: 12, of which 4 were waited for; matrix products, arithmetic and copies ran while one was open for 1% of the time, Pallas kernels for 13%

profile of v4, /device:TPU:0, one launch (start us, length us, event | category | flops | bytes accessed | tf_op | source)
XLA Modules:
  0.0 53.6 jit_solution(11985412466099478936)
XLA Ops:
  0.1 1.3 %copy-done.1 = bf16[8,2,64,512]{3,2,1,0:T(8,128)(2,1)S(1)} copy-done((bf16[8,2,64,512]{3,2,1,0:T(8,128)(2,1)S(1)}, bf16[8,2,64,512]{3,2,1,0:T(8,128)(2,1)}, u32[]{:S(2)}) %copy-start.1) | copy-done | bytes 1048600
  1.4 0.7 %edges.1 = (bf16[8,24,512]{2,1,0:T(8,128)(2,1)S(1)}, bf16[8,24,512]{2,1,0:T(8,128)(2,1)S(1)}) custom-call(s32[4]{0:T(128)S(1)} %pad_add_fusion.place_ref, bf16[8,2,64,512]{3,2,1,0:T(8,128)(2,1)S(1)} %copy-done.1), custom_call_target="tpu_custom_call" | custom-call | tf_op jit(solution)/shard_map/edges/pallas_call | solution.py:69
  2.0 0.7 %collective-permute-start = (bf16[8,24,512]{2,1,0:T(8,128)(2,1)S(1)}, bf16[8,24,512]{2,1,0:T(8,128)(2,1)S(1)}, u32[]{:S(2)}, u32[]{:S(2)}) collective-permute-start(bf16[8,24,512]{2,1,0:T(8,128)(2,1)S(1)} %get-tuple-element.19), channel_id=1, source_target_pairs={{1,2},{3,4},{5,6},{2,1},{4,3},{6,5},{9,10},{11,12},{13,14},{10,9},... | collective-permute-start | bytes 589832 | tf_op jit(solution)/shard_map/ppermute | solution.py:429
  2.7 5.8 %collective-permute-start.1 = (bf16[8,24,512]{2,1,0:T(8,128)(2,1)S(1)}, bf16[8,24,512]{2,1,0:T(8,128)(2,1)S(1)}, u32[]{:S(2)}, u32[]{:S(2)}) collective-permute-start(bf16[8,24,512]{2,1,0:T(8,128)(2,1)S(1)} %get-tuple-element.20), channel_id=1, source_target_pairs={{0,1},{1,0},{2,3},{3,2},{4,5},{5,4},{6,7},{7,6},{8,9},{9,8},{10,11... | collective-permute-start | bytes 589832 | tf_op jit(solution)/shard_map/ppermute | solution.py:430
  8.5 0.6 %copy-done.2 = s32[32,1]{0,1:T(1,128)S(1)} copy-done((s32[32,1]{0,1:T(1,128)S(1)}, s32[32,1]{0,1:T(1,128)}, u32[]{:S(2)}) %copy-start.2) | copy-done | bytes 152
  9.2 0.6 %pack_weights.2 = (bf16[528,128]{1,0:T(8,128)(2,1)S(1)}, bf16[528,128]{1,0:T(8,128)(2,1)S(1)}, bf16[528,128]{1,0:T(8,128)(2,1)S(1)}) custom-call(s32[4]{0:T(128)S(1)} %pad_add_fusion.place_ref, bf16[32,16384]{1,0:T(8,128)(2,1)S(1)} %copy-done, s32[1,32]{1,0:T(1,128)S(1)} %bitcast.6, s32[1,32]{1,0:T(1,128)S(1)} %bitcast.8), custom_call_target="tpu_custom_call" | custom-call | tf_op jit(solution)/shard_map/pack_weights/pallas_call | solution.py:100
  9.8 1.6 %collective-permute-start.5 = (bf16[528,128]{1,0:T(8,128)(2,1)S(1)}, bf16[528,128]{1,0:T(8,128)(2,1)S(1)}, u32[]{:S(2)}, u32[]{:S(2)}) collective-permute-start(bf16[528,128]{1,0:T(8,128)(2,1)S(1)} %get-tuple-element.25), channel_id=1, source_target_pairs={{0,2},{1,3},{2,0},{3,1},{4,6},{5,7},{6,4},{7,5},{8,10},{9,11},{10,... | collective-permute-start | bytes 405512 | tf_op jit(solution)/shard_map/ppermute | solution.py:434
  11.5 2.5 %collective-permute-start.6 = (bf16[528,128]{1,0:T(8,128)(2,1)S(1)}, bf16[528,128]{1,0:T(8,128)(2,1)S(1)}, u32[]{:S(2)}, u32[]{:S(2)}) collective-permute-start(bf16[528,128]{1,0:T(8,128)(2,1)S(1)} %get-tuple-element.26), channel_id=1, source_target_pairs={{0,6},{1,7},{2,4},{3,5},{4,2},{5,3},{6,0},{7,1},{8,14},{9,15},{10,... | collective-permute-start | bytes 405512 | tf_op jit(solution)/shard_map/ppermute | solution.py:434
  14.0 0.7 %pack_weights.3 = (bf16[528,128]{1,0:T(8,128)(2,1)S(1)}, bf16[528,128]{1,0:T(8,128)(2,1)S(1)}, bf16[528,128]{1,0:T(8,128)(2,1)S(1)}, bf16[528,128]{1,0:T(8,128)(2,1)S(1)}, bf16[528,128]{1,0:T(8,128)(2,1)S(1)}) custom-call(s32[4]{0:T(128)S(1)} %pad_add_fusion.place_ref, bf16[32,16384]{1,0:T(8,128)(2,1)S(1)} %copy-done, s32[1,32]{1,0:T(1,128)S(1)} %bitcast.7, ...), custom_call_target="tpu_custom_call" | custom-call | tf_op jit(solution)/shard_map/pack_weights/pallas_call | solution.py:100
  14.7 1.7 %collective-permute-start.8 = (bf16[528,128]{1,0:T(8,128)(2,1)S(1)}, bf16[528,128]{1,0:T(8,128)(2,1)S(1)}, u32[]{:S(2)}, u32[]{:S(2)}) collective-permute-start(bf16[528,128]{1,0:T(8,128)(2,1)S(1)} %get-tuple-element.28), channel_id=1, source_target_pairs={{0,1},{1,0},{2,3},{3,2},{4,5},{5,4},{6,7},{7,6},{8,9},{9,8},{10,11... | collective-permute-start | bytes 405512 | tf_op jit(solution)/shard_map/ppermute | solution.py:434
  16.4 3.6 %collective-permute-start.9 = (bf16[528,128]{1,0:T(8,128)(2,1)S(1)}, bf16[528,128]{1,0:T(8,128)(2,1)S(1)}, u32[]{:S(2)}, u32[]{:S(2)}) collective-permute-start(bf16[528,128]{1,0:T(8,128)(2,1)S(1)} %get-tuple-element.29), channel_id=1, source_target_pairs={{0,7},{1,6},{2,5},{3,4},{4,3},{5,2},{6,1},{7,0},{8,15},{9,14},{10,... | collective-permute-start | bytes 405512 | tf_op jit(solution)/shard_map/ppermute | solution.py:434
  20.0 3.3 %smooth.1 = (bf16[8,2,64,128]{3,2,1,0:T(8,128)(2,1)S(1)}, bf16[8,2,64,128]{3,2,1,0:T(8,128)(2,1)S(1)}, bf16[8,2,64,128]{3,2,1,0:T(8,128)(2,1)S(1)}, bf16[8,2,64,128]{3,2,1,0:T(8,128)(2,1)S(1)}) custom-call(s32[2,8]{1,0:T(2,128)S(1)} %bitcast.10, s32[4]{0:T(128)S(1)} %pad_add_fusion.place_ref, bf16[8,2,64,512]{3,2,1,0:T(8,128)(2,1)S(1)} %copy-done.1, ...), custom_call_target="tpu_custom_call" | custom-call | tf_op jit(solution)/shard_map/smooth/pallas_call | solution.py:206
  23.3 0.7 %collective-permute-start.2 = (bf16[8,2,64,128]{3,2,1,0:T(8,128)(2,1)S(1)}, bf16[8,2,64,128]{3,2,1,0:T(8,128)(2,1)S(1)}, u32[]{:S(2)}, u32[]{:S(2)}) collective-permute-start(bf16[8,2,64,128]{3,2,1,0:T(8,128)(2,1)S(1)} %get-tuple-element.21), channel_id=1, source_target_pairs={{0,24},{8,16},{16,8},{24,0},{1,25},{9,17},{17,9},{25,1},{2,26},{10... | collective-permute-start | bytes 786440 | tf_op jit(solution)/shard_map/ppermute | solution.py:439
  24.0 1.0 %collective-permute-start.3 = (bf16[8,2,64,128]{3,2,1,0:T(8,128)(2,1)S(1)}, bf16[8,2,64,128]{3,2,1,0:T(8,128)(2,1)S(1)}, u32[]{:S(2)}, u32[]{:S(2)}) collective-permute-start(bf16[8,2,64,128]{3,2,1,0:T(8,128)(2,1)S(1)} %get-tuple-element.22), channel_id=1, source_target_pairs={{0,16},{8,24},{16,0},{24,8},{1,17},{9,25},{17,1},{25,9},{2,18},{10... | collective-permute-start | bytes 786440 | tf_op jit(solution)/shard_map/ppermute | solution.py:439
  25.0 4.2 %collective-permute-done.7.refs_6_.refs_2_ = bf16[528,128]{1,0:T(8,128)(2,1)S(1)} collective-permute-done((bf16[528,128]{1,0:T(8,128)(2,1)S(1)}, bf16[528,128]{1,0:T(8,128)(2,1)S(1)}, u32[]{:S(2)}, u32[]{:S(2)}) %collective-permute-start.7) | collective-permute-done | bytes 135200 | tf_op jit(solution)/shard_map/ppermute | solution.py:434
  29.5 1.3 %collective-permute-start.10 = (bf16[528,128]{1,0:T(8,128)(2,1)S(1)}, bf16[528,128]{1,0:T(8,128)(2,1)S(1)}, u32[]{:S(2)}, u32[]{:S(2)}) collective-permute-start(bf16[528,128]{1,0:T(8,128)(2,1)S(1)} %get-tuple-element.30), channel_id=1, source_target_pairs={{0,5},{1,4},{2,7},{3,6},{4,1},{5,0},{6,3},{7,2},{8,13},{9,12},{10,... | collective-permute-start | bytes 405512 | tf_op jit(solution)/shard_map/ppermute | solution.py:434
  30.8 2.2 %collective-permute-start.11 = (bf16[528,128]{1,0:T(8,128)(2,1)S(1)}, bf16[528,128]{1,0:T(8,128)(2,1)S(1)}, u32[]{:S(2)}, u32[]{:S(2)}) collective-permute-start(bf16[528,128]{1,0:T(8,128)(2,1)S(1)} %get-tuple-element.31), channel_id=1, source_target_pairs={{0,3},{1,2},{2,1},{3,0},{4,7},{5,6},{6,5},{7,4},{8,11},{9,10},{10,... | collective-permute-start | bytes 405512 | tf_op jit(solution)/shard_map/ppermute | solution.py:434
  33.3 1.2 %spread_filters.1.spread_ref = bf16[2,512,512]{2,1,0:T(8,128)(2,1)S(1)} custom-call(s32[4]{0:T(128)S(1)} %pad_add_fusion.place_ref, bf16[2,32,32]{2,1,0:T(8,128)(2,1)S(1)} %multiply_reduce_fusion.kernel_ref), custom_call_target="tpu_custom_call" | custom-call | tf_op jit(solution)/shard_map/spread_filters/pallas_call | solution.py:244
  34.5 3.1 %collective-permute-done.3.refs_1_ = bf16[8,2,64,128]{3,2,1,0:T(8,128)(2,1)S(1)} collective-permute-done((bf16[8,2,64,128]{3,2,1,0:T(8,128)(2,1)S(1)}, bf16[8,2,64,128]{3,2,1,0:T(8,128)(2,1)S(1)}, u32[]{:S(2)}, u32[]{:S(2)}) %collective-permute-start.3) | collective-permute-done | bytes 262176 | tf_op jit(solution)/shard_map/ppermute | solution.py:439
  37.6 1.2 %deconvolve.1.spikes_ref = bf16[1,16,256,128]{3,2,1,0:T(8,128)(2,1)S(1)} custom-call(bf16[2,512,512]{2,1,0:T(8,128)(2,1)S(1)} %spread_filters.1.spread_ref, bf16[8,2,64,128]{3,2,1,0:T(8,128)(2,1)S(1)} %collective-permute-done.2.refs_0_, bf16[8,2,64,128]{3,2,1,0:T(8,128)(2,1)S(1)} %collective-permute-done.3.refs_1_, ...), custom_call_target="tpu_custom_call" | custom-call | tf_op jit(solution)/shard_map/deconvolve/pallas_call | solution.py:311
  38.9 1.1 %collective-permute-done.10.refs_5_ = bf16[528,128]{1,0:T(8,128)(2,1)S(1)} collective-permute-done((bf16[528,128]{1,0:T(8,128)(2,1)S(1)}, bf16[528,128]{1,0:T(8,128)(2,1)S(1)}, u32[]{:S(2)}, u32[]{:S(2)}) %collective-permute-start.10) | collective-permute-done | bytes 135200 | tf_op jit(solution)/shard_map/ppermute | solution.py:434
  40.3 1.4 %pool.1 = f32[32,8,128]{2,1,0:T(8,128)S(1)} custom-call(s32[4]{0:T(128)S(1)} %pad_add_fusion.place_ref, bf16[1,16,256,128]{3,2,1,0:T(8,128)(2,1)S(1)} %deconvolve.1.spikes_ref, bf16[528,128]{1,0:T(8,128)(2,1)S(1)} %collective-permute-done.5.refs_4_.refs_0_, bf16[528,128]{1,0:T(8,128)(2,1)S(1)} %collective-permute-done.6.refs_5_.refs_1_, ...), custom_call_target="tpu_custom_call" | custom-call | tf_op jit(solution)/shard_map/pool/pallas_call | solution.py:386
  41.8 11.1 %all_to_all.5.parts_ref = f32[32,8,128]{2,1,0:T(8,128)S(1)} all-to-all(f32[32,8,128]{2,1,0:T(8,128)S(1)} %pool.1), channel_id=1, replica_groups=mesh['frame'=4,'tile'=8] {'frame','tile'}, dimensions={0} | all-to-all | bytes 262144 | tf_op jit(solution)/shard_map/all_to_all | solution.py:443
  52.9 0.7 %finish.1 = f32[32,32]{1,0:T(8,128)} custom-call(f32[32,8,128]{2,1,0:T(8,128)S(1)} %all_to_all.5.parts_ref), custom_call_target="tpu_custom_call" | custom-call | tf_op jit(solution)/shard_map/finish/pallas_call | solution.py:405
  (25 shorter events, 1.1 us)
Async XLA Ops:
  0.0 8.5 %copy-start = (bf16[32,16384]{1,0:T(8,128)(2,1)S(1)}, bf16[32,16384]{1,0:T(8,128)(2,1)}, u32[]{:S(2)}) copy-start(bf16[32,16384]{1,0:T(8,128)(2,1)} %weights_ref.3) | copy-start | bytes 3145732
  0.1 1.3 %copy-start.1 = (bf16[8,2,64,512]{3,2,1,0:T(8,128)(2,1)S(1)}, bf16[8,2,64,512]{3,2,1,0:T(8,128)(2,1)}, u32[]{:S(2)}) copy-start(bf16[8,2,64,512]{3,2,1,0:T(8,128)(2,1)} %movie_ref.3) | copy-start | bytes 3145732
  2.0 11.9 %collective-permute-start = (bf16[8,24,512]{2,1,0:T(8,128)(2,1)S(1)}, bf16[8,24,512]{2,1,0:T(8,128)(2,1)S(1)}, u32[]{:S(2)}, u32[]{:S(2)}) collective-permute-start(bf16[8,24,512]{2,1,0:T(8,128)(2,1)S(1)} %get-tuple-element.19), channel_id=1, source_target_pairs={{1,2},{3,4},{5,6},{2,1},{4,3},{6,5},{9,10},{11,12},{13,14},{10,9},... | collective-permute-start | bytes 589832 | tf_op jit(solution)/shard_map/ppermute | solution.py:429
  2.7 13.7 %collective-permute-start.1 = (bf16[8,24,512]{2,1,0:T(8,128)(2,1)S(1)}, bf16[8,24,512]{2,1,0:T(8,128)(2,1)S(1)}, u32[]{:S(2)}, u32[]{:S(2)}) collective-permute-start(bf16[8,24,512]{2,1,0:T(8,128)(2,1)S(1)} %get-tuple-element.20), channel_id=1, source_target_pairs={{0,1},{1,0},{2,3},{3,2},{4,5},{5,4},{6,7},{7,6},{8,9},{9,8},{10,11... | collective-permute-start | bytes 589832 | tf_op jit(solution)/shard_map/ppermute | solution.py:430
  8.5 0.7 %copy-start.2 = (s32[32,1]{0,1:T(1,128)S(1)}, s32[32,1]{0,1:T(1,128)}, u32[]{:S(2)}) copy-start(s32[32,1]{0,1:T(1,128)} %param.10) | copy-start | bytes 388
  8.5 0.7 %copy-start.3 = (s32[32,1]{0,1:T(1,128)S(1)}, s32[32,1]{0,1:T(1,128)}, u32[]{:S(2)}) copy-start(s32[32,1]{0,1:T(1,128)} %param.11) | copy-start | bytes 388
  9.8 13.5 %collective-permute-start.5 = (bf16[528,128]{1,0:T(8,128)(2,1)S(1)}, bf16[528,128]{1,0:T(8,128)(2,1)S(1)}, u32[]{:S(2)}, u32[]{:S(2)}) collective-permute-start(bf16[528,128]{1,0:T(8,128)(2,1)S(1)} %get-tuple-element.25), channel_id=1, source_target_pairs={{0,2},{1,3},{2,0},{3,1},{4,6},{5,7},{6,4},{7,5},{8,10},{9,11},{10,... | collective-permute-start | bytes 405512 | tf_op jit(solution)/shard_map/ppermute | solution.py:434
  11.5 12.5 %collective-permute-start.6 = (bf16[528,128]{1,0:T(8,128)(2,1)S(1)}, bf16[528,128]{1,0:T(8,128)(2,1)S(1)}, u32[]{:S(2)}, u32[]{:S(2)}) collective-permute-start(bf16[528,128]{1,0:T(8,128)(2,1)S(1)} %get-tuple-element.26), channel_id=1, source_target_pairs={{0,6},{1,7},{2,4},{3,5},{4,2},{5,3},{6,0},{7,1},{8,14},{9,15},{10,... | collective-permute-start | bytes 405512 | tf_op jit(solution)/shard_map/ppermute | solution.py:434
  14.0 15.3 %collective-permute-start.7 = (bf16[528,128]{1,0:T(8,128)(2,1)S(1)}, bf16[528,128]{1,0:T(8,128)(2,1)S(1)}, u32[]{:S(2)}, u32[]{:S(2)}) collective-permute-start(bf16[528,128]{1,0:T(8,128)(2,1)S(1)} %get-tuple-element.27), channel_id=1, source_target_pairs={{0,4},{1,5},{2,6},{3,7},{4,0},{5,1},{6,2},{7,3},{8,12},{9,13},{10,... | collective-permute-start | bytes 405512 | tf_op jit(solution)/shard_map/ppermute | solution.py:434
  14.7 14.8 %collective-permute-start.8 = (bf16[528,128]{1,0:T(8,128)(2,1)S(1)}, bf16[528,128]{1,0:T(8,128)(2,1)S(1)}, u32[]{:S(2)}, u32[]{:S(2)}) collective-permute-start(bf16[528,128]{1,0:T(8,128)(2,1)S(1)} %get-tuple-element.28), channel_id=1, source_target_pairs={{0,1},{1,0},{2,3},{3,2},{4,5},{5,4},{6,7},{7,6},{8,9},{9,8},{10,11... | collective-permute-start | bytes 405512 | tf_op jit(solution)/shard_map/ppermute | solution.py:434
  16.4 3.6 %copy-start.4 = (s32[8,2]{0,1:T(2,128)S(1)}, s32[8,2]{0,1:T(2,128)}, u32[]{:S(2)}) copy-start(s32[8,2]{0,1:T(2,128)} %param.7) | copy-start | bytes 196
  16.4 14.4 %collective-permute-start.9 = (bf16[528,128]{1,0:T(8,128)(2,1)S(1)}, bf16[528,128]{1,0:T(8,128)(2,1)S(1)}, u32[]{:S(2)}, u32[]{:S(2)}) collective-permute-start(bf16[528,128]{1,0:T(8,128)(2,1)S(1)} %get-tuple-element.29), channel_id=1, source_target_pairs={{0,7},{1,6},{2,5},{3,4},{4,3},{5,2},{6,1},{7,0},{8,15},{9,14},{10,... | collective-permute-start | bytes 405512 | tf_op jit(solution)/shard_map/ppermute | solution.py:434
  23.3 11.2 %collective-permute-start.2 = (bf16[8,2,64,128]{3,2,1,0:T(8,128)(2,1)S(1)}, bf16[8,2,64,128]{3,2,1,0:T(8,128)(2,1)S(1)}, u32[]{:S(2)}, u32[]{:S(2)}) collective-permute-start(bf16[8,2,64,128]{3,2,1,0:T(8,128)(2,1)S(1)} %get-tuple-element.21), channel_id=1, source_target_pairs={{0,24},{8,16},{16,8},{24,0},{1,25},{9,17},{17,9},{25,1},{2,26},{10... | collective-permute-start | bytes 786440 | tf_op jit(solution)/shard_map/ppermute | solution.py:439
  24.0 13.6 %collective-permute-start.3 = (bf16[8,2,64,128]{3,2,1,0:T(8,128)(2,1)S(1)}, bf16[8,2,64,128]{3,2,1,0:T(8,128)(2,1)S(1)}, u32[]{:S(2)}, u32[]{:S(2)}) collective-permute-start(bf16[8,2,64,128]{3,2,1,0:T(8,128)(2,1)S(1)} %get-tuple-element.22), channel_id=1, source_target_pairs={{0,16},{8,24},{16,0},{24,8},{1,17},{9,25},{17,1},{25,9},{2,18},{10... | collective-permute-start | bytes 786440 | tf_op jit(solution)/shard_map/ppermute | solution.py:439
  29.2 8.4 %collective-permute-start.4 = (bf16[8,2,64,128]{3,2,1,0:T(8,128)(2,1)S(1)}, bf16[8,2,64,128]{3,2,1,0:T(8,128)(2,1)S(1)}, u32[]{:S(2)}, u32[]{:S(2)}) collective-permute-start(bf16[8,2,64,128]{3,2,1,0:T(8,128)(2,1)S(1)} %get-tuple-element.23), channel_id=1, source_target_pairs={{0,8},{8,0},{16,24},{24,16},{1,9},{9,1},{17,25},{25,17},{2,10},{10... | collective-permute-start | bytes 786440 | tf_op jit(solution)/shard_map/ppermute | solution.py:439
  29.5 3.5 %copy-start.5 = (f32[2,64]{1,0:T(2,128)S(1)}, f32[2,64]{1,0:T(2,128)}, u32[]{:S(2)}) copy-start(f32[2,64]{1,0:T(2,128)} %param.8) | copy-start | bytes 1540
  29.5 10.5 %collective-permute-start.10 = (bf16[528,128]{1,0:T(8,128)(2,1)S(1)}, bf16[528,128]{1,0:T(8,128)(2,1)S(1)}, u32[]{:S(2)}, u32[]{:S(2)}) collective-permute-start(bf16[528,128]{1,0:T(8,128)(2,1)S(1)} %get-tuple-element.30), channel_id=1, source_target_pairs={{0,5},{1,4},{2,7},{3,6},{4,1},{5,0},{6,3},{7,2},{8,13},{9,12},{10,... | collective-permute-start | bytes 405512 | tf_op jit(solution)/shard_map/ppermute | solution.py:434
  30.8 9.5 %collective-permute-start.11 = (bf16[528,128]{1,0:T(8,128)(2,1)S(1)}, bf16[528,128]{1,0:T(8,128)(2,1)S(1)}, u32[]{:S(2)}, u32[]{:S(2)}) collective-permute-start(bf16[528,128]{1,0:T(8,128)(2,1)S(1)} %get-tuple-element.31), channel_id=1, source_target_pairs={{0,3},{1,2},{2,1},{3,0},{4,7},{5,6},{6,5},{7,4},{8,11},{9,10},{10,... | collective-permute-start | bytes 405512 | tf_op jit(solution)/shard_map/ppermute | solution.py:434

commit v5 on v4

--- a/solution.py
+++ b/solution.py
@@ -422,7 +422,7 @@
     tile = lax.axis_index("tile")
     place = jnp.stack([tile * rows, tiles * rows, lax.axis_index("frame"), tile]).astype(jnp.int32)
     far, close = list(range(tiles // 2, tiles)), list(range(1, tiles // 2))
-    order = close[1:2] + far[-2:-1] + far[:1] + close[:1] + far[-1:] + far[-3:0:-1] + close[2:] + [0]
+    order = close[1:2] + far[-2:] + far[:1] + close[:1] + far[-3:0:-1] + close[2:] + [0]
     owner, local = slot_owner.reshape(1, slots), slot_local.reshape(1, slots)
     pair, other = edges(movie, place)
     swaps = [(i, i + 1) for i in range(1, ends, 2)]

time: 53.8 us -> 53.8 us (level)
  waiting for transfers between devices: 8.76 us -> 10.9 us
  starting transfers between devices: 21 us -> 19.7 us
  blocking collectives: 11.1 us -> 10.4 us
    ppermute x7, waiting for transfers between devices: 5.67 us -> 9.91 us  [body(): lax.ppermute(cells, 'tile', [(i, i ^ k) for i in range(tiles)])]
    ppermute x3, waiting for transfers between devices: 3.09 us -> 0.95 us  [body(): lax.ppermute(pieces[k], 'frame', [(i, i ^ k) for i in range(parts)])]
    ppermute x7, starting transfers between devices: 12.9 us -> 11.3 us  [body(): lax.ppermute(cells, 'tile', [(i, i ^ k) for i in range(tiles)])]
    all_to_all x1, blocking collectives: 11.1 us -> 10.4 us  [body(): lax.all_to_all(traces, ('frame', 'tile'), split_axis=0, concat_axis=0, ti...]
where the time goes in v5:
time: 53.8 us; the launch traced here: 53.6 us
  starting transfers between devices  19.7 us (37%)
  waiting for transfers between devices  10.9 us (20%)
  blocking collectives  10.4 us (19%)
  Pallas kernels  9.97 us (19%)
  local copies, waits for them, and re-layouts  1.98 us (4%)
  other arithmetic  0.64 us (1%)
    ppermute x7, starting transfers between devices, body(): lax.ppermute(cells, 'tile', [(i, i ^ k) for i in range(tiles)])  11.3 us
    all_to_all x1, blocking collectives, body(): lax.all_to_all(traces, ('frame', 'tile'), split_axis=0, concat_axis=0, ti...  10.4 us
    ppermute x7, waiting for transfers between devices, body(): lax.ppermute(cells, 'tile', [(i, i ^ k) for i in range(tiles)])  9.91 us
    ppermute x1, starting transfers between devices, body(): pair = lax.ppermute(pair, 'tile', [(i, i ^ 1) for i in range(tiles)])  5.79 us
    pallas_call x1, Pallas kernels, smooth(): pl.pallas_call(smooth_kernel, out_shape=[jax.ShapeDtypeStruct((frames, pl...  3.34 us
    unnamed x12, local copies, waits for them, and re-layouts  1.98 us
    ppermute x3, starting transfers between devices, body(): lax.ppermute(pieces[k], 'frame', [(i, i ^ k) for i in range(parts)])  1.93 us
    pallas_call x1, Pallas kernels, pool(): pl.pallas_call(functools.partial(pool_kernel, order), out_shape=jax.Shape...  1.44 us
  transfers between devices with their start and end apart: 12, of which 4 were waited for; matrix products, arithmetic and copies ran while one was open for 1% of the time, Pallas kernels for 13%

profile of v5, /device:TPU:0, one launch (start us, length us, event | category | flops | bytes accessed | tf_op | source)
XLA Modules:
  0.0 53.6 jit_solution(9725182318806402724)
XLA Ops:
  0.1 1.3 %copy-done.1 = bf16[8,2,64,512]{3,2,1,0:T(8,128)(2,1)S(1)} copy-done((bf16[8,2,64,512]{3,2,1,0:T(8,128)(2,1)S(1)}, bf16[8,2,64,512]{3,2,1,0:T(8,128)(2,1)}, u32[]{:S(2)}) %copy-start.1) | copy-done | bytes 1048600
  1.4 0.7 %edges.1 = (bf16[8,24,512]{2,1,0:T(8,128)(2,1)S(1)}, bf16[8,24,512]{2,1,0:T(8,128)(2,1)S(1)}) custom-call(s32[4]{0:T(128)S(1)} %pad_add_fusion.place_ref, bf16[8,2,64,512]{3,2,1,0:T(8,128)(2,1)S(1)} %copy-done.1), custom_call_target="tpu_custom_call" | custom-call | tf_op jit(solution)/shard_map/edges/pallas_call | solution.py:69
  2.0 0.7 %collective-permute-start = (bf16[8,24,512]{2,1,0:T(8,128)(2,1)S(1)}, bf16[8,24,512]{2,1,0:T(8,128)(2,1)S(1)}, u32[]{:S(2)}, u32[]{:S(2)}) collective-permute-start(bf16[8,24,512]{2,1,0:T(8,128)(2,1)S(1)} %get-tuple-element.19), channel_id=1, source_target_pairs={{1,2},{3,4},{5,6},{2,1},{4,3},{6,5},{9,10},{11,12},{13,14},{10,9},... | collective-permute-start | bytes 589832 | tf_op jit(solution)/shard_map/ppermute | solution.py:429
  2.7 5.8 %collective-permute-start.1 = (bf16[8,24,512]{2,1,0:T(8,128)(2,1)S(1)}, bf16[8,24,512]{2,1,0:T(8,128)(2,1)S(1)}, u32[]{:S(2)}, u32[]{:S(2)}) collective-permute-start(bf16[8,24,512]{2,1,0:T(8,128)(2,1)S(1)} %get-tuple-element.20), channel_id=1, source_target_pairs={{0,1},{1,0},{2,3},{3,2},{4,5},{5,4},{6,7},{7,6},{8,9},{9,8},{10,11... | collective-permute-start | bytes 589832 | tf_op jit(solution)/shard_map/ppermute | solution.py:430
  8.5 0.6 %copy-done.2 = s32[32,1]{0,1:T(1,128)S(1)} copy-done((s32[32,1]{0,1:T(1,128)S(1)}, s32[32,1]{0,1:T(1,128)}, u32[]{:S(2)}) %copy-start.2) | copy-done | bytes 152
  9.2 0.6 %pack_weights.2 = (bf16[528,128]{1,0:T(8,128)(2,1)S(1)}, bf16[528,128]{1,0:T(8,128)(2,1)S(1)}, bf16[528,128]{1,0:T(8,128)(2,1)S(1)}) custom-call(s32[4]{0:T(128)S(1)} %pad_add_fusion.place_ref, bf16[32,16384]{1,0:T(8,128)(2,1)S(1)} %copy-done, s32[1,32]{1,0:T(1,128)S(1)} %bitcast.6, s32[1,32]{1,0:T(1,128)S(1)} %bitcast.8), custom_call_target="tpu_custom_call" | custom-call | tf_op jit(solution)/shard_map/pack_weights/pallas_call | solution.py:100
  9.8 1.6 %collective-permute-start.5 = (bf16[528,128]{1,0:T(8,128)(2,1)S(1)}, bf16[528,128]{1,0:T(8,128)(2,1)S(1)}, u32[]{:S(2)}, u32[]{:S(2)}) collective-permute-start(bf16[528,128]{1,0:T(8,128)(2,1)S(1)} %get-tuple-element.25), channel_id=1, source_target_pairs={{0,2},{1,3},{2,0},{3,1},{4,6},{5,7},{6,4},{7,5},{8,10},{9,11},{10,... | collective-permute-start | bytes 405512 | tf_op jit(solution)/shard_map/ppermute | solution.py:434
  11.5 2.5 %collective-permute-start.6 = (bf16[528,128]{1,0:T(8,128)(2,1)S(1)}, bf16[528,128]{1,0:T(8,128)(2,1)S(1)}, u32[]{:S(2)}, u32[]{:S(2)}) collective-permute-start(bf16[528,128]{1,0:T(8,128)(2,1)S(1)} %get-tuple-element.26), channel_id=1, source_target_pairs={{0,6},{1,7},{2,4},{3,5},{4,2},{5,3},{6,0},{7,1},{8,14},{9,15},{10,... | collective-permute-start | bytes 405512 | tf_op jit(solution)/shard_map/ppermute | solution.py:434
  14.0 1.1 %collective-permute-start.7 = (bf16[528,128]{1,0:T(8,128)(2,1)S(1)}, bf16[528,128]{1,0:T(8,128)(2,1)S(1)}, u32[]{:S(2)}, u32[]{:S(2)}) collective-permute-start(bf16[528,128]{1,0:T(8,128)(2,1)S(1)} %get-tuple-element.27), channel_id=1, source_target_pairs={{0,7},{1,6},{2,5},{3,4},{4,3},{5,2},{6,1},{7,0},{8,15},{9,14},{10,... | collective-permute-start | bytes 405512 | tf_op jit(solution)/shard_map/ppermute | solution.py:434
  15.1 0.7 %pack_weights.3 = (bf16[528,128]{1,0:T(8,128)(2,1)S(1)}, bf16[528,128]{1,0:T(8,128)(2,1)S(1)}, bf16[528,128]{1,0:T(8,128)(2,1)S(1)}, bf16[528,128]{1,0:T(8,128)(2,1)S(1)}, bf16[528,128]{1,0:T(8,128)(2,1)S(1)}) custom-call(s32[4]{0:T(128)S(1)} %pad_add_fusion.place_ref, bf16[32,16384]{1,0:T(8,128)(2,1)S(1)} %copy-done, s32[1,32]{1,0:T(1,128)S(1)} %bitcast.7, ...), custom_call_target="tpu_custom_call" | custom-call | tf_op jit(solution)/shard_map/pack_weights/pallas_call | solution.py:100
  15.8 0.9 %collective-permute-start.8 = (bf16[528,128]{1,0:T(8,128)(2,1)S(1)}, bf16[528,128]{1,0:T(8,128)(2,1)S(1)}, u32[]{:S(2)}, u32[]{:S(2)}) collective-permute-start(bf16[528,128]{1,0:T(8,128)(2,1)S(1)} %get-tuple-element.28), channel_id=1, source_target_pairs={{0,4},{1,5},{2,6},{3,7},{4,0},{5,1},{6,2},{7,3},{8,12},{9,13},{10,... | collective-permute-start | bytes 405512 | tf_op jit(solution)/shard_map/ppermute | solution.py:434
  16.7 2.4 %collective-permute-start.9 = (bf16[528,128]{1,0:T(8,128)(2,1)S(1)}, bf16[528,128]{1,0:T(8,128)(2,1)S(1)}, u32[]{:S(2)}, u32[]{:S(2)}) collective-permute-start(bf16[528,128]{1,0:T(8,128)(2,1)S(1)} %get-tuple-element.29), channel_id=1, source_target_pairs={{0,1},{1,0},{2,3},{3,2},{4,5},{5,4},{6,7},{7,6},{8,9},{9,8},{10,11... | collective-permute-start | bytes 405512 | tf_op jit(solution)/shard_map/ppermute | solution.py:434
  19.1 3.3 %smooth.1 = (bf16[8,2,64,128]{3,2,1,0:T(8,128)(2,1)S(1)}, bf16[8,2,64,128]{3,2,1,0:T(8,128)(2,1)S(1)}, bf16[8,2,64,128]{3,2,1,0:T(8,128)(2,1)S(1)}, bf16[8,2,64,128]{3,2,1,0:T(8,128)(2,1)S(1)}) custom-call(s32[2,8]{1,0:T(2,128)S(1)} %bitcast.10, s32[4]{0:T(128)S(1)} %pad_add_fusion.place_ref, bf16[8,2,64,512]{3,2,1,0:T(8,128)(2,1)S(1)} %copy-done.1, ...), custom_call_target="tpu_custom_call" | custom-call | tf_op jit(solution)/shard_map/smooth/pallas_call | solution.py:206
  22.4 0.5 collective-permute-start.2
  22.9 1.2 %collective-permute-start.3 = (bf16[8,2,64,128]{3,2,1,0:T(8,128)(2,1)S(1)}, bf16[8,2,64,128]{3,2,1,0:T(8,128)(2,1)S(1)}, u32[]{:S(2)}, u32[]{:S(2)}) collective-permute-start(bf16[8,2,64,128]{3,2,1,0:T(8,128)(2,1)S(1)} %get-tuple-element.22), channel_id=1, source_target_pairs={{0,16},{8,24},{16,0},{24,8},{1,17},{9,25},{17,1},{25,9},{2,18},{10... | collective-permute-start | bytes 786440 | tf_op jit(solution)/shard_map/ppermute | solution.py:439
  24.6 6.8 %collective-permute-done.8.refs_7_.refs_3_ = bf16[528,128]{1,0:T(8,128)(2,1)S(1)} collective-permute-done((bf16[528,128]{1,0:T(8,128)(2,1)S(1)}, bf16[528,128]{1,0:T(8,128)(2,1)S(1)}, u32[]{:S(2)}, u32[]{:S(2)}) %collective-permute-start.8) | collective-permute-done | bytes 135200 | tf_op jit(solution)/shard_map/ppermute | solution.py:434
  31.6 2.6 %collective-permute-start.11 = (bf16[528,128]{1,0:T(8,128)(2,1)S(1)}, bf16[528,128]{1,0:T(8,128)(2,1)S(1)}, u32[]{:S(2)}, u32[]{:S(2)}) collective-permute-start(bf16[528,128]{1,0:T(8,128)(2,1)S(1)} %get-tuple-element.31), channel_id=1, source_target_pairs={{0,3},{1,2},{2,1},{3,0},{4,7},{5,6},{6,5},{7,4},{8,11},{9,10},{10,... | collective-permute-start | bytes 405512 | tf_op jit(solution)/shard_map/ppermute | solution.py:434
  34.6 1.2 %spread_filters.1.spread_ref = bf16[2,512,512]{2,1,0:T(8,128)(2,1)S(1)} custom-call(s32[4]{0:T(128)S(1)} %pad_add_fusion.place_ref, bf16[2,32,32]{2,1,0:T(8,128)(2,1)S(1)} %multiply_reduce_fusion.kernel_ref), custom_call_target="tpu_custom_call" | custom-call | tf_op jit(solution)/shard_map/spread_filters/pallas_call | solution.py:244
  35.8 0.9 %collective-permute-done.3.refs_1_ = bf16[8,2,64,128]{3,2,1,0:T(8,128)(2,1)S(1)} collective-permute-done((bf16[8,2,64,128]{3,2,1,0:T(8,128)(2,1)S(1)}, bf16[8,2,64,128]{3,2,1,0:T(8,128)(2,1)S(1)}, u32[]{:S(2)}, u32[]{:S(2)}) %collective-permute-start.3) | collective-permute-done | bytes 262176 | tf_op jit(solution)/shard_map/ppermute | solution.py:439
  36.7 1.2 %deconvolve.1.spikes_ref = bf16[1,16,256,128]{3,2,1,0:T(8,128)(2,1)S(1)} custom-call(bf16[2,512,512]{2,1,0:T(8,128)(2,1)S(1)} %spread_filters.1.spread_ref, bf16[8,2,64,128]{3,2,1,0:T(8,128)(2,1)S(1)} %collective-permute-done.2.refs_0_, bf16[8,2,64,128]{3,2,1,0:T(8,128)(2,1)S(1)} %collective-permute-done.3.refs_1_, ...), custom_call_target="tpu_custom_call" | custom-call | tf_op jit(solution)/shard_map/deconvolve/pallas_call | solution.py:311
  38.0 2.8 %collective-permute-done.10.refs_5_ = bf16[528,128]{1,0:T(8,128)(2,1)S(1)} collective-permute-done((bf16[528,128]{1,0:T(8,128)(2,1)S(1)}, bf16[528,128]{1,0:T(8,128)(2,1)S(1)}, u32[]{:S(2)}, u32[]{:S(2)}) %collective-permute-start.10) | collective-permute-done | bytes 135200 | tf_op jit(solution)/shard_map/ppermute | solution.py:434
  41.1 1.4 %pool.1 = f32[32,8,128]{2,1,0:T(8,128)S(1)} custom-call(s32[4]{0:T(128)S(1)} %pad_add_fusion.place_ref, bf16[1,16,256,128]{3,2,1,0:T(8,128)(2,1)S(1)} %deconvolve.1.spikes_ref, bf16[528,128]{1,0:T(8,128)(2,1)S(1)} %collective-permute-done.5.refs_4_.refs_0_, bf16[528,128]{1,0:T(8,128)(2,1)S(1)} %collective-permute-done.6.refs_5_.refs_1_, ...), custom_call_target="tpu_custom_call" | custom-call | tf_op jit(solution)/shard_map/pool/pallas_call | solution.py:386
  42.5 10.4 %all_to_all.5.parts_ref = f32[32,8,128]{2,1,0:T(8,128)S(1)} all-to-all(f32[32,8,128]{2,1,0:T(8,128)S(1)} %pool.1), channel_id=1, replica_groups=mesh['frame'=4,'tile'=8] {'frame','tile'}, dimensions={0} | all-to-all | bytes 262144 | tf_op jit(solution)/shard_map/all_to_all | solution.py:443
  52.9 0.7 %finish.1 = f32[32,32]{1,0:T(8,128)} custom-call(f32[32,8,128]{2,1,0:T(8,128)S(1)} %all_to_all.5.parts_ref), custom_call_target="tpu_custom_call" | custom-call | tf_op jit(solution)/shard_map/finish/pallas_call | solution.py:405
  (25 shorter events, 1.4 us)
Async XLA Ops:
  0.0 8.5 %copy-start = (bf16[32,16384]{1,0:T(8,128)(2,1)S(1)}, bf16[32,16384]{1,0:T(8,128)(2,1)}, u32[]{:S(2)}) copy-start(bf16[32,16384]{1,0:T(8,128)(2,1)} %weights_ref.3) | copy-start | bytes 3145732
  0.1 1.3 %copy-start.1 = (bf16[8,2,64,512]{3,2,1,0:T(8,128)(2,1)S(1)}, bf16[8,2,64,512]{3,2,1,0:T(8,128)(2,1)}, u32[]{:S(2)}) copy-start(bf16[8,2,64,512]{3,2,1,0:T(8,128)(2,1)} %movie_ref.3) | copy-start | bytes 3145732
  2.0 13.1 %collective-permute-start = (bf16[8,24,512]{2,1,0:T(8,128)(2,1)S(1)}, bf16[8,24,512]{2,1,0:T(8,128)(2,1)S(1)}, u32[]{:S(2)}, u32[]{:S(2)}) collective-permute-start(bf16[8,24,512]{2,1,0:T(8,128)(2,1)S(1)} %get-tuple-element.19), channel_id=1, source_target_pairs={{1,2},{3,4},{5,6},{2,1},{4,3},{6,5},{9,10},{11,12},{13,14},{10,9},... | collective-permute-start | bytes 589832 | tf_op jit(solution)/shard_map/ppermute | solution.py:429
  2.7 14.0 %collective-permute-start.1 = (bf16[8,24,512]{2,1,0:T(8,128)(2,1)S(1)}, bf16[8,24,512]{2,1,0:T(8,128)(2,1)S(1)}, u32[]{:S(2)}, u32[]{:S(2)}) collective-permute-start(bf16[8,24,512]{2,1,0:T(8,128)(2,1)S(1)} %get-tuple-element.20), channel_id=1, source_target_pairs={{0,1},{1,0},{2,3},{3,2},{4,5},{5,4},{6,7},{7,6},{8,9},{9,8},{10,11... | collective-permute-start | bytes 589832 | tf_op jit(solution)/shard_map/ppermute | solution.py:430
  8.5 0.7 %copy-start.2 = (s32[32,1]{0,1:T(1,128)S(1)}, s32[32,1]{0,1:T(1,128)}, u32[]{:S(2)}) copy-start(s32[32,1]{0,1:T(1,128)} %param.10) | copy-start | bytes 388
  8.5 0.7 %copy-start.3 = (s32[32,1]{0,1:T(1,128)S(1)}, s32[32,1]{0,1:T(1,128)}, u32[]{:S(2)}) copy-start(s32[32,1]{0,1:T(1,128)} %param.11) | copy-start | bytes 388
  9.8 12.6 %collective-permute-start.5 = (bf16[528,128]{1,0:T(8,128)(2,1)S(1)}, bf16[528,128]{1,0:T(8,128)(2,1)S(1)}, u32[]{:S(2)}, u32[]{:S(2)}) collective-permute-start(bf16[528,128]{1,0:T(8,128)(2,1)S(1)} %get-tuple-element.25), channel_id=1, source_target_pairs={{0,2},{1,3},{2,0},{3,1},{4,6},{5,7},{6,4},{7,5},{8,10},{9,11},{10,... | collective-permute-start | bytes 405512 | tf_op jit(solution)/shard_map/ppermute | solution.py:434
  11.5 11.4 %collective-permute-start.6 = (bf16[528,128]{1,0:T(8,128)(2,1)S(1)}, bf16[528,128]{1,0:T(8,128)(2,1)S(1)}, u32[]{:S(2)}, u32[]{:S(2)}) collective-permute-start(bf16[528,128]{1,0:T(8,128)(2,1)S(1)} %get-tuple-element.26), channel_id=1, source_target_pairs={{0,6},{1,7},{2,4},{3,5},{4,2},{5,3},{6,0},{7,1},{8,14},{9,15},{10,... | collective-permute-start | bytes 405512 | tf_op jit(solution)/shard_map/ppermute | solution.py:434
  14.0 10.2 %collective-permute-start.7 = (bf16[528,128]{1,0:T(8,128)(2,1)S(1)}, bf16[528,128]{1,0:T(8,128)(2,1)S(1)}, u32[]{:S(2)}, u32[]{:S(2)}) collective-permute-start(bf16[528,128]{1,0:T(8,128)(2,1)S(1)} %get-tuple-element.27), channel_id=1, source_target_pairs={{0,7},{1,6},{2,5},{3,4},{4,3},{5,2},{6,1},{7,0},{8,15},{9,14},{10,... | collective-permute-start | bytes 405512 | tf_op jit(solution)/shard_map/ppermute | solution.py:434
  15.8 15.5 %collective-permute-start.8 = (bf16[528,128]{1,0:T(8,128)(2,1)S(1)}, bf16[528,128]{1,0:T(8,128)(2,1)S(1)}, u32[]{:S(2)}, u32[]{:S(2)}) collective-permute-start(bf16[528,128]{1,0:T(8,128)(2,1)S(1)} %get-tuple-element.28), channel_id=1, source_target_pairs={{0,4},{1,5},{2,6},{3,7},{4,0},{5,1},{6,2},{7,3},{8,12},{9,13},{10,... | collective-permute-start | bytes 405512 | tf_op jit(solution)/shard_map/ppermute | solution.py:434
  16.7 2.4 %copy-start.4 = (s32[8,2]{0,1:T(2,128)S(1)}, s32[8,2]{0,1:T(2,128)}, u32[]{:S(2)}) copy-start(s32[8,2]{0,1:T(2,128)} %param.7) | copy-start | bytes 196
  16.7 14.9 %collective-permute-start.9 = (bf16[528,128]{1,0:T(8,128)(2,1)S(1)}, bf16[528,128]{1,0:T(8,128)(2,1)S(1)}, u32[]{:S(2)}, u32[]{:S(2)}) collective-permute-start(bf16[528,128]{1,0:T(8,128)(2,1)S(1)} %get-tuple-element.29), channel_id=1, source_target_pairs={{0,1},{1,0},{2,3},{3,2},{4,5},{5,4},{6,7},{7,6},{8,9},{9,8},{10,11... | collective-permute-start | bytes 405512 | tf_op jit(solution)/shard_map/ppermute | solution.py:434
  22.4 13.3 %collective-permute-start.2 = (bf16[8,2,64,128]{3,2,1,0:T(8,128)(2,1)S(1)}, bf16[8,2,64,128]{3,2,1,0:T(8,128)(2,1)S(1)}, u32[]{:S(2)}, u32[]{:S(2)}) collective-permute-start(bf16[8,2,64,128]{3,2,1,0:T(8,128)(2,1)S(1)} %get-tuple-element.21), channel_id=1, source_target_pairs={{0,24},{8,16},{16,8},{24,0},{1,25},{9,17},{17,9},{25,1},{2,26},{10... | collective-permute-start | bytes 786440 | tf_op jit(solution)/shard_map/ppermute | solution.py:439
  22.9 13.8 %collective-permute-start.3 = (bf16[8,2,64,128]{3,2,1,0:T(8,128)(2,1)S(1)}, bf16[8,2,64,128]{3,2,1,0:T(8,128)(2,1)S(1)}, u32[]{:S(2)}, u32[]{:S(2)}) collective-permute-start(bf16[8,2,64,128]{3,2,1,0:T(8,128)(2,1)S(1)} %get-tuple-element.22), channel_id=1, source_target_pairs={{0,16},{8,24},{16,0},{24,8},{1,17},{9,25},{17,1},{25,9},{2,18},{10... | collective-permute-start | bytes 786440 | tf_op jit(solution)/shard_map/ppermute | solution.py:439
  24.1 12.6 %collective-permute-start.4 = (bf16[8,2,64,128]{3,2,1,0:T(8,128)(2,1)S(1)}, bf16[8,2,64,128]{3,2,1,0:T(8,128)(2,1)S(1)}, u32[]{:S(2)}, u32[]{:S(2)}) collective-permute-start(bf16[8,2,64,128]{3,2,1,0:T(8,128)(2,1)S(1)} %get-tuple-element.23), channel_id=1, source_target_pairs={{0,8},{8,0},{16,24},{24,16},{1,9},{9,1},{17,25},{25,17},{2,10},{10... | collective-permute-start | bytes 786440 | tf_op jit(solution)/shard_map/ppermute | solution.py:439
  31.4 2.8 %copy-start.5 = (f32[2,64]{1,0:T(2,128)S(1)}, f32[2,64]{1,0:T(2,128)}, u32[]{:S(2)}) copy-start(f32[2,64]{1,0:T(2,128)} %param.8) | copy-start | bytes 1540
  31.4 9.3 %collective-permute-start.10 = (bf16[528,128]{1,0:T(8,128)(2,1)S(1)}, bf16[528,128]{1,0:T(8,128)(2,1)S(1)}, u32[]{:S(2)}, u32[]{:S(2)}) collective-permute-start(bf16[528,128]{1,0:T(8,128)(2,1)S(1)} %get-tuple-element.30), channel_id=1, source_target_pairs={{0,5},{1,4},{2,7},{3,6},{4,1},{5,0},{6,3},{7,2},{8,13},{9,12},{10,... | collective-permute-start | bytes 405512 | tf_op jit(solution)/shard_map/ppermute | solution.py:434
  31.6 9.5 %collective-permute-start.11 = (bf16[528,128]{1,0:T(8,128)(2,1)S(1)}, bf16[528,128]{1,0:T(8,128)(2,1)S(1)}, u32[]{:S(2)}, u32[]{:S(2)}) collective-permute-start(bf16[528,128]{1,0:T(8,128)(2,1)S(1)} %get-tuple-element.31), channel_id=1, source_target_pairs={{0,3},{1,2},{2,1},{3,0},{4,7},{5,6},{6,5},{7,4},{8,11},{9,10},{10,... | collective-permute-start | bytes 405512 | tf_op jit(solution)/shard_map/ppermute | solution.py:434
